TPU v7x, 32 devices: a whole 2x2x4 slice. The times are simulated.
32 devices in a mesh: section: 2 (over x), dp: 16 (over z, y, core).
Axes of the slice: x: 2, y: 2, z: 4, core: 2. Of those that a mesh axis runs over, the one named last changes fastest.
Arguments:
- tokens: bfloat16 [64, 256, 640], P('dp'), may hold values from -6 to 6
- lengths: int32 [64], P('dp'), may hold values from 64 to 256
- cotangent: bfloat16 [64, 256, 640], P('dp'), may hold values from -6 to 6
- w_qkv: bfloat16 [2, 640, 1920], P('section', 'dp'), may hold values from -0.25 to 0.25
- w_out: bfloat16 [2, 640, 640], P('section', 'dp'), may hold values from -1 to 1
- w_up: bfloat16 [2, 640, 5120], P('section', 'dp'), may hold values from -0.25 to 0.25
- w_down: bfloat16 [2, 5120, 640], P('section', 'dp'), may hold values from -0.078125 to 0.078125
- norm_gain: bfloat16 [2, 2, 640], P('section', None, 'dp'), may hold values from 0.25 to 1.75
- norm_bias: bfloat16 [2, 2, 640], P('section', None, 'dp'), may hold values from -1 to 1
- bias_vec: bfloat16 [2, 4, 640], P('section', None, 'dp'), may hold values from -1 to 1
- up_bias: bfloat16 [2, 5120], P('section', 'dp'), may hold values from -1 to 1
Outputs:
- hidden_out: bfloat16 [2, 64, 256, 640], P('section', 'dp')
- input_grads: float32 [2, 64, 256, 640], P('section', 'dp')
- grad_qkv: float32 [2, 640, 1920], P('section', 'dp')
- grad_out: float32 [2, 640, 640], P('section', 'dp')
- grad_up: float32 [2, 640, 5120], P('section', 'dp')
- grad_down: float32 [2, 5120, 640], P('section', 'dp')
- grad_gain: float32 [2, 2, 640], P('section', None, 'dp')
- grad_norm_bias: float32 [2, 2, 640], P('section', None, 'dp')
- grad_bias_vec: float32 [2, 4, 640], P('section', None, 'dp')
- grad_up_bias: float32 [2, 5120], P('section', 'dp')
All inputs are finite; a program needn't handle non-finite values.
Results may differ from a plain program's by a relative error of at most 0.015.
Values may be sent and summed in bfloat16 or wider, within the bound.
No kernel may reach another device: no remote copies, remote signals or barrier semaphores. Data moves between devices by JAX's collectives and lax.ppermute only.
A program may use at most 320 MiB of HBM per device.

v0:
```python
import jax
import jax.numpy as jnp
from jax import lax
from jax.experimental import pallas as pl
from jax.experimental.pallas import tpu as pltpu
from jax.sharding import PartitionSpec as P

HEADS = 20
HEAD_DIM = 32
GROUP = 128 // HEAD_DIM
SCALE = HEAD_DIM ** -0.5
LOG2E = 1.4426950408889634
VMEM_LIMIT = 56 * 1024 * 1024
F32 = jnp.float32
BF16 = jnp.bfloat16


def cost(us):
    return pl.CostEstimate(flops=int(us * 1.1e9), bytes_accessed=1024, transcendentals=0)


def tied(count):
    return [pl.BlockSpec(memory_space=pl.ANY)] * count


def dot(a, b, dims=((1,), (0,))):
    return lax.dot_general(a, b, (dims, ((), ())), preferred_element_type=F32)


def gelu_pair(u):
    below = 0.5 + 0.5 * lax.erf(u * 0.7071067811865476)
    return u * below, below + (0.3989422804014327 * u) * jnp.exp(-0.5 * (u * u))


def normed(v, gain, shift):
    centered = v - jnp.mean(v, axis=-1, keepdims=True)
    spread = jnp.mean(centered * centered, axis=-1, keepdims=True)
    hat = centered * lax.rsqrt(spread + 1e-05)
    return hat * gain + shift


def norm_back(v, gain, grad):
    centered = v - jnp.mean(v, axis=-1, keepdims=True)
    spread = jnp.mean(centered * centered, axis=-1, keepdims=True)
    inv = lax.rsqrt(spread + 1e-05)
    hat = centered * inv
    g = grad * gain
    back = inv * (g - jnp.mean(g, axis=-1, keepdims=True) - hat * jnp.mean(g * hat, axis=-1, keepdims=True))
    return back, jnp.sum(grad * hat, axis=0, keepdims=True), jnp.sum(grad, axis=0, keepdims=True)


def attn_fwd_body(save, first_window, len_ref, h_ref, *rest):
    if save:
        arrived_ref, wqkv_ref, vec_ref, m_ref, c_ref, qkv_ref, e_ref, o_ref, a_ref, inv_ref, taken_ref = rest
    else:
        wqkv_ref, m_ref, c_ref = rest
    width = h_ref.shape[2]
    seq = h_ref.shape[1]
    length = len_ref[pl.program_id(0) + first_window]
    if save:
        taken = jnp.where(len_ref[len_ref.shape[0] - 1] == 0, h_ref[0], arrived_ref[0])
        taken_ref[0] = taken
        h = taken.astype(F32)
        vec = vec_ref[...]
    else:
        h = h_ref[0].astype(F32)
        vec = wqkv_ref[:, 4 * width:].astype(F32).T
    a = normed(h, vec[0:1], vec[2:3]).astype(BF16)
    q_all = (dot(a, wqkv_ref[:, :width]) + vec[4:5]).astype(BF16)
    k_all = dot(a, wqkv_ref[:, width:2 * width]).astype(BF16)
    v_all = (dot(a, wqkv_ref[:, 2 * width:3 * width]) + vec[5:6]).astype(BF16)
    if save:
        a_ref[0] = a
        qkv_ref[0, :, :width] = q_all
        qkv_ref[0, :, width:2 * width] = k_all
        qkv_ref[0, :, 2 * width:] = v_all
    head_of = lax.broadcasted_iota(jnp.int32, (1, 128), 1) // HEAD_DIM
    key_at = lax.broadcasted_iota(jnp.int32, (seq, 128), 0)
    lane = lax.broadcasted_iota(jnp.int32, (seq, 128), 1)
    past = jnp.where((lane == 0) & (key_at >= length), -1e30, 0.0).astype(BF16)
    first = jnp.where(lane == 0, 1.0, 0.0).astype(BF16)
    ones = jnp.ones((seq, 128), BF16)
    zero = jnp.zeros((seq, 128), BF16)
    mixed = []
    for g in range(width // 128):
        at = slice(128 * g, 128 * g + 128)
        q, v = q_all[:, at], v_all[:, at]
        k = jnp.concatenate([k_all[:, at], past], axis=1)
        acc, inv = None, None
        stacked = dot(jnp.concatenate([jnp.concatenate([jnp.where(head_of == j, q, zero), first], axis=1) for j in range(GROUP)], axis=0), k, ((1,), (1,)))
        for j in range(GROUP):
            mine = head_of == j
            s = stacked[seq * j:seq * j + seq]
            e = jnp.exp2((s - jnp.max(s, axis=1, keepdims=True)) * (SCALE * LOG2E)).astype(BF16)
            if save:
                e_ref[0, GROUP * g + j] = e
            both_parts = dot(e, jnp.concatenate([jnp.where(mine, v, zero), ones], axis=1))
            one_over = 1.0 / both_parts[:, 128:]
            part = both_parts[:, :128] * one_over
            acc = part if acc is None else acc + part
            inv = one_over if inv is None else jnp.where(mine, one_over, inv)
        mixed.append(acc.astype(BF16))
        if save:
            inv_ref[0, :, at] = inv
    o = jnp.concatenate(mixed, axis=1)
    if save:
        o_ref[0] = o
    m = h + dot(o, wqkv_ref[:, 3 * width:4 * width]) + vec[6:7]
    m_ref[0] = m
    c_ref[0] = normed(m, vec[1:2], vec[3:4]).astype(BF16)


def whole(shape):
    return pl.BlockSpec(shape, lambda *_: (0,) * len(shape))


def attn_fwd(h, lengths, proj, save, at=0, parts=1, arrived=None, vec=None, earlier=(), after=()):
    n, seq, width = h.shape
    count = n // parts
    row = lambda *tail: pl.BlockSpec((1,) + tail, lambda i, *_: (i + at * count,) + (0,) * len(tail))
    shapes = [((seq, width), F32), ((seq, width), BF16)]
    args, in_specs = [h], [row(seq, width)]
    if save:
        shapes += [((seq, 3 * width), BF16), ((HEADS, seq, seq), BF16), ((seq, width), BF16), ((seq, width), BF16), ((seq, width), F32), ((seq, width), BF16)]
        args += [arrived, proj, vec]
        in_specs += [pl.BlockSpec((1, seq, width), lambda i, *_: (i, 0, 0)), whole(proj.shape), whole(vec.shape)]
    else:
        args += [proj]
        in_specs += [whole(proj.shape)]
    used, waits = 1 + len(args), len(earlier) + len(after)
    return pl.pallas_call(
        lambda *refs: attn_fwd_body(save, at * count, *refs[:used], *refs[used + waits:]),
        grid_spec=pltpu.PrefetchScalarGridSpec(
            num_scalar_prefetch=1,
            grid=(count,),
            in_specs=in_specs + tied(waits),
            out_specs=[row(*s) for s, _ in shapes],
        ),
        out_shape=[jax.ShapeDtypeStruct((n,) + s, d) for s, d in shapes],
        input_output_aliases={used + i: i for i in range(len(earlier))},
        compiler_params=pltpu.CompilerParams(vmem_limit_bytes=VMEM_LIMIT),
        cost_estimate=cost(4.5 * count),
        name="attention_forward",
    )(lengths, *args, *earlier, *after)


def mlp_fwd_body(save, rows, c_ref, m_ref, wup_ref, wdown_ref, bup_ref, vec_ref, *outs):
    if save:
        y_ref, g_ref, gp_ref, acc_ref = outs
    else:
        y_ref, acc_ref = outs
    step = pl.program_id(0)

    @pl.when(step == 0)
    def _():
        acc_ref[...] = m_ref[...] + vec_ref[7:8]

    for r in range(c_ref.shape[0] // rows):
        at = slice(r * rows, r * rows + rows)
        u = dot(c_ref[at], wup_ref[...]) + bup_ref[...]
        act, slope = gelu_pair(u)
        act = act.astype(BF16)
        if save:
            g_ref[at] = act
            gp_ref[at] = slope.astype(BF16)
        acc_ref[at] += dot(act, wdown_ref[...])

    @pl.when(step == pl.num_programs(0) - 1)
    def _():
        y_ref[...] = acc_ref[...].astype(BF16)


def mlp_fwd(c, m, wup, wdown, bup, vec, save, at=0, parts=1, after=(), chunk=1280, rows=256):
    n, width = c.shape
    n //= parts
    waits = len(after)
    part = pl.BlockSpec((n, width), lambda i: (at, 0))
    ff = wup.shape[1]
    outs = [jax.ShapeDtypeStruct((n, width), BF16)]
    specs = [whole((n, width))]
    if save:
        outs += [jax.ShapeDtypeStruct((n, ff), BF16)] * 2
        specs += [pl.BlockSpec((n, chunk), lambda i: (0, i))] * 2
    return pl.pallas_call(
        lambda *refs: mlp_fwd_body(save, rows, *refs[:6], *refs[6 + waits:]),
        grid=(ff // chunk,),
        in_specs=[part, part, pl.BlockSpec((width, chunk), lambda i: (0, i)),
                  pl.BlockSpec((chunk, width), lambda i: (i, 0)), pl.BlockSpec((1, chunk), lambda i: (0, i)), whole(vec.shape)] + tied(waits),
        out_specs=specs,
        out_shape=outs,
        scratch_shapes=[pltpu.VMEM((n, width), F32)],
        compiler_params=pltpu.CompilerParams(vmem_limit_bytes=VMEM_LIMIT),
        cost_estimate=cost(26),
        name="feed_forward",
    )(c, m, wup, wdown, bup, vec, *after)


def mlp_both_body(rows, c_ref, m_ref, dz_ref, wup_ref, wdown_ref, bup_ref, vec_ref, y_ref, g_ref, gp_ref, dc_ref, acc_ref):
    step = pl.program_id(0)

    @pl.when(step == 0)
    def _():
        acc_ref[...] = m_ref[...] + vec_ref[7:8]
        dc_ref[...] = jnp.zeros_like(dc_ref)

    for r in range(c_ref.shape[0] // rows):
        at = slice(r * rows, r * rows + rows)
        u = dot(c_ref[at], wup_ref[...]) + bup_ref[...]
        dg = dot(dz_ref[at], wdown_ref[...], ((1,), (1,)))
        act, slope = gelu_pair(u)
        act, slope = act.astype(BF16), slope.astype(BF16)
        g_ref[at] = act
        gp_ref[at] = slope
        acc_ref[at] += dot(act, wdown_ref[...])
        dc_ref[at] += dot((dg * slope.astype(F32)).astype(BF16), wup_ref[...], ((1,), (1,)))

    @pl.when(step == pl.num_programs(0) - 1)
    def _():
        y_ref[...] = acc_ref[...].astype(BF16)


def mlp_both(c, m, dz, wup, wdown, bup, vec, chunk=1280, rows=256):
    n, width = c.shape
    ff = wup.shape[1]
    column = pl.BlockSpec((n, chunk), lambda i: (0, i))
    return pl.pallas_call(
        lambda *refs: mlp_both_body(rows, *refs),
        grid=(ff // chunk,),
        in_specs=[whole(c.shape), whole(m.shape), whole(dz.shape), pl.BlockSpec((width, chunk), lambda i: (0, i)),
                  pl.BlockSpec((chunk, width), lambda i: (i, 0)), pl.BlockSpec((1, chunk), lambda i: (0, i)), whole(vec.shape)],
        out_specs=[whole((n, width)), column, column, whole((n, width))],
        out_shape=[jax.ShapeDtypeStruct((n, width), BF16), jax.ShapeDtypeStruct((n, ff), BF16), jax.ShapeDtypeStruct((n, ff), BF16),
                   jax.ShapeDtypeStruct((n, width), F32)],
        scratch_shapes=[pltpu.VMEM((n, width), F32)],
        compiler_params=pltpu.CompilerParams(vmem_limit_bytes=VMEM_LIMIT),
        cost_estimate=cost(42),
        name="feed_forward_both",
    )(c, m, dz, wup, wdown, bup, vec)


def mlp_up_body(rows, c_ref, wup_ref, bup_ref, g_ref):
    for r in range(c_ref.shape[0] // rows):
        at = slice(r * rows, r * rows + rows)
        g_ref[at] = gelu_pair(dot(c_ref[at], wup_ref[...]) + bup_ref[...])[0].astype(BF16)


def mlp_up(c, wup, bup, at=0, parts=1, after=(), chunk=1280, rows=256):
    n, width = c.shape
    n //= parts
    ff = wup.shape[1]
    waits = len(after)
    return pl.pallas_call(
        lambda *refs: mlp_up_body(rows, *refs[:3], *refs[3 + waits:]),
        grid=(ff // chunk,),
        in_specs=[pl.BlockSpec((n, width), lambda i: (at, 0)), pl.BlockSpec((width, chunk), lambda i: (0, i)), pl.BlockSpec((1, chunk), lambda i: (0, i))] + tied(waits),
        out_specs=pl.BlockSpec((n, chunk), lambda i: (0, i)),
        out_shape=jax.ShapeDtypeStruct((n, ff), BF16),
        compiler_params=pltpu.CompilerParams(vmem_limit_bytes=VMEM_LIMIT),
        cost_estimate=cost(0.0125 * n),
        name="feed_forward_up",
    )(c, wup, bup, *after)


def mlp_down_body(g_ref, m_ref, wdown_ref, vec_ref, y_ref, acc_ref):
    step = pl.program_id(0)

    @pl.when(step == 0)
    def _():
        acc_ref[...] = m_ref[...] + vec_ref[7:8]

    acc_ref[...] += dot(g_ref[...], wdown_ref[...])

    @pl.when(step == pl.num_programs(0) - 1)
    def _():
        y_ref[...] = acc_ref[...].astype(BF16)


def mlp_down(g, m, wdown, vec, at, parts, after=(), chunk=1280):
    ff, width = wdown.shape
    rows = g.shape[0] // parts
    waits = len(after)
    return pl.pallas_call(
        lambda *refs: mlp_down_body(*refs[:4], *refs[4 + waits:]),
        grid=(ff // chunk,),
        in_specs=[pl.BlockSpec((rows, chunk), lambda i: (at, i)), pl.BlockSpec((rows, width), lambda i: (at, 0)),
                  pl.BlockSpec((chunk, width), lambda i: (i, 0)), whole(vec.shape)] + tied(waits),
        out_specs=whole((rows, width)),
        out_shape=jax.ShapeDtypeStruct((rows, width), BF16),
        scratch_shapes=[pltpu.VMEM((rows, width), F32)],
        compiler_params=pltpu.CompilerParams(vmem_limit_bytes=VMEM_LIMIT),
        cost_estimate=cost(0.017 * rows),
        name="feed_forward_down",
    )(g, m, wdown, vec, *after)


def mlp_bwd_body(save, rows, dz_ref, gp_ref, wup_ref, wdown_ref, dc_ref, *outs):
    @pl.when(pl.program_id(0) == 0)
    def _():
        dc_ref[...] = jnp.zeros_like(dc_ref)

    for r in range(dz_ref.shape[0] // rows):
        at = slice(r * rows, r * rows + rows)
        dg = dot(dz_ref[at], wdown_ref[...], ((1,), (1,)))
        du = (dg * gp_ref[at].astype(F32)).astype(BF16)
        if save:
            outs[0][at] = du
        dc_ref[at] += dot(du, wup_ref[...], ((1,), (1,)))


def mlp_bwd(dz, gp, wup, wdown, save, at=0, parts=1, earlier=(), after=(), chunk=1280, rows=256):
    n, width = dz.shape
    ff = wup.shape[1]
    args = [dz, gp, wup, wdown, *earlier, *after]
    outs = [jax.ShapeDtypeStruct((n * parts, width), F32)]
    specs = [pl.BlockSpec((n, width), lambda i: (at, 0))]
    if save:
        outs += [jax.ShapeDtypeStruct((n, ff), BF16)]
        specs += [pl.BlockSpec((n, chunk), lambda i: (0, i))]
    return pl.pallas_call(
        lambda *refs: mlp_bwd_body(save, rows, *refs[:4], *refs[len(args):]),
        grid=(ff // chunk,),
        in_specs=[whole(dz.shape), pl.BlockSpec((n, chunk), lambda i: (at, i)), pl.BlockSpec((width, chunk), lambda i: (0, i)),
                  pl.BlockSpec((chunk, width), lambda i: (i, 0))] + tied(len(args) - 4),
        out_specs=specs,
        out_shape=outs,
        input_output_aliases={4 + i: i for i in range(len(earlier))},
        compiler_params=pltpu.CompilerParams(vmem_limit_bytes=VMEM_LIMIT),
        cost_estimate=cost(22 / parts),
        name="feed_forward_back",
    )(*args)


def up_grad_body(c_ref, order_ref, du_ref, keep_ref, send_ref, sum_ref, ct_ref):
    half = keep_ref.shape[0]

    @pl.when(pl.program_id(0) == 0)
    def _():
        ct_ref[:2 * half] = dot(order_ref[...], c_ref[...], ((1,), (1,))).astype(BF16)
        ct_ref[2 * half:] = jnp.ones_like(ct_ref[2 * half:])

    grad = dot(ct_ref[...], du_ref[...])
    keep_ref[...] = grad[:half].astype(BF16)
    send_ref[...] = grad[half:2 * half].astype(BF16)
    sum_ref[...] = grad[2 * half:2 * half + 8]


def up_grad(c, order, du, at, parts, after=(), chunk=1280):
    n, width = c.shape
    ff = du.shape[1] // parts
    first = at * ff // chunk
    waits = len(after)
    column = lambda rows: pl.BlockSpec((rows, chunk), lambda i: (0, i))
    return pl.pallas_call(
        lambda *refs: up_grad_body(*refs[:3], *refs[3 + waits:]),
        grid=(ff // chunk,),
        in_specs=[whole(c.shape), whole(order.shape), pl.BlockSpec((n, chunk), lambda i: (0, i + first))] + tied(waits),
        out_specs=[column(width // 2), column(width // 2), column(8)],
        out_shape=[jax.ShapeDtypeStruct((width // 2, ff), BF16)] * 2 + [jax.ShapeDtypeStruct((8, ff), F32)],
        scratch_shapes=[pltpu.VMEM((width + 16, n), BF16)],
        compiler_params=pltpu.CompilerParams(vmem_limit_bytes=VMEM_LIMIT),
        cost_estimate=cost(13 / parts),
        name="up_gradient",
    )(c, order, du, *after)


def mlp_grad_body(rows, dz_ref, gp_ref, wup_ref, wdown_ref, early_ref, c_ref, order_ref, dc_ref, keep_ref, send_ref, sum_ref, du_ref, ct_ref):
    half = keep_ref.shape[0]
    count = early_ref.shape[0]

    @pl.when(pl.program_id(0) == 0)
    def _():
        dc_ref[...] = jnp.zeros_like(dc_ref)
        ct_ref[:2 * half] = dot(order_ref[...], c_ref[...], ((1,), (1,))).astype(BF16)
        ct_ref[2 * half:] = jnp.ones_like(ct_ref[2 * half:])

    for r in range(dz_ref.shape[0] // rows):
        at = slice(r * rows, r * rows + rows)
        dg = dot(dz_ref[at], wdown_ref[...], ((1,), (1,)))
        du = (dg * gp_ref[at].astype(F32)).astype(BF16)
        du_ref[at] = du
        dc_ref[at] += dot(du, wup_ref[...], ((1,), (1,)))
    grad = dot(ct_ref[:, :count], early_ref[...]) + dot(ct_ref[:, count:], du_ref[...])
    keep_ref[...] = grad[:half].astype(BF16)
    send_ref[...] = grad[half:2 * half].astype(BF16)
    sum_ref[...] = grad[2 * half:2 * half + 8]


def mlp_grad(dz, gp, wup, wdown, early, c, order, dc, after=(), chunk=1280, rows=256):
    count, width = dz.shape
    n, ff = gp.shape
    at = n // count - 1
    waits = 1 + len(after)
    column = lambda rows: pl.BlockSpec((rows, chunk), lambda i: (0, i))
    return pl.pallas_call(
        lambda *refs: mlp_grad_body(rows, *refs[:7], *refs[7 + waits:]),
        grid=(ff // chunk,),
        in_specs=[whole(dz.shape), pl.BlockSpec((count, chunk), lambda i: (at, i)), column(width), pl.BlockSpec((chunk, width), lambda i: (i, 0)),
                  column(n - count), whole(c.shape), whole(order.shape)] + tied(waits),
        out_specs=[pl.BlockSpec((count, width), lambda i: (at, 0)), column(width // 2), column(width // 2), column(8)],
        out_shape=[jax.ShapeDtypeStruct((n, width), F32)] + [jax.ShapeDtypeStruct((width // 2, ff), BF16)] * 2 + [jax.ShapeDtypeStruct((8, ff), F32)],
        scratch_shapes=[pltpu.VMEM((count, chunk), BF16), pltpu.VMEM((width + 16, n), BF16)],
        input_output_aliases={7: 0},
        compiler_params=pltpu.CompilerParams(vmem_limit_bytes=VMEM_LIMIT),
        cost_estimate=cost(21),
        name="feed_forward_gradients",
    )(dz, gp, wup, wdown, early, c, order, dc, *after)


def down_grad_body(g_ref, dz_ref, out_ref):
    out_ref[...] = dot(g_ref[...], dz_ref[...], ((0,), (0,))).astype(BF16)


def down_grad(g, dz, after=(), chunk=1280):
    n, ff = g.shape
    width = dz.shape[1]
    waits = len(after)
    return pl.pallas_call(
        lambda *refs: down_grad_body(*refs[:2], *refs[2 + waits:]),
        grid=(ff // chunk,),
        in_specs=[pl.BlockSpec((n, chunk), lambda i: (0, i)), whole(dz.shape)] + tied(waits),
        out_specs=pl.BlockSpec((chunk, width), lambda i: (i, 0)),
        out_shape=jax.ShapeDtypeStruct((ff, width), BF16),
        compiler_params=pltpu.CompilerParams(vmem_limit_bytes=VMEM_LIMIT),
        cost_estimate=cost(12),
        name="down_gradient",
    )(g, dz, *after)


def attn_bwd_body(grads, base_ref, dc_ref, dz_ref, m_ref, h_ref, qkv_ref, e_ref, o_ref, inv_ref, proj_ref, vec_ref, dh_ref, *outs):
    if grads:
        dr_ref, dqkv_ref, small_ref = outs
    width = h_ref.shape[2]
    vec = vec_ref[...]

    if grads:
        @pl.when(pl.program_id(0) == 0)
        def _():
            small_ref[...] = jnp.zeros_like(small_ref) if base_ref is None else base_ref[...]

    dz = dz_ref[0].astype(F32)
    back, g_gain1, g_shift1 = norm_back(m_ref[0], vec[1:2], dc_ref[0])
    dm = dz + back
    dr = dm.astype(BF16)
    if grads:
        dr_ref[0] = dr
    do_all = dot(dr, proj_ref[:, 3 * width:4 * width], ((1,), (1,))).astype(BF16)
    seq = h_ref.shape[1]
    head_of = lax.broadcasted_iota(jnp.int32, (1, 128), 1) // HEAD_DIM
    ones = jnp.ones((seq, 128), BF16)
    zero = jnp.zeros((seq, 128), BF16)
    dq_all, dk_all, dv_all = [], [], []
    for g in range(width // 128):
        at = slice(128 * g, 128 * g + 128)
        q = qkv_ref[0, :, 128 * g:128 * g + 128]
        k = qkv_ref[0, :, width + 128 * g:width + 128 * g + 128]
        v = jnp.concatenate([qkv_ref[0, :, 2 * width + 128 * g:2 * width + 128 * g + 128], ones], axis=1)
        scaled = do_all[:, at].astype(F32) * (inv_ref[0, :, at] * SCALE)
        do = scaled.astype(BF16)
        less = (-scaled * o_ref[0, :, at].astype(F32)).astype(BF16)
        do_t, q_t = do.T, q.T
        dq = None
        dk_t, dv_t = [], []
        stacked = dot(jnp.concatenate([jnp.concatenate([jnp.where(head_of == j, do, zero), jnp.where(head_of == j, less, zero)], axis=1)
                                       for j in range(GROUP)], axis=0), v, ((1,), (1,)))
        for j in range(GROUP):
            mine = head_of == j
            e = e_ref[0, GROUP * g + j]
            rows = slice(HEAD_DIM * j, HEAD_DIM * j + HEAD_DIM)
            dv_t.append(dot(do_t[rows], e))
            dp = stacked[seq * j:seq * j + seq]
            ds = (e.astype(F32) * dp).astype(BF16)
            part = dot(ds, jnp.where(mine, k, zero))
            dq = part if dq is None else dq + part
            dk_t.append(dot(q_t[rows], ds))
        dq_all.append(dq.astype(BF16))
        dk_all.append(jnp.concatenate(dk_t, axis=0).astype(BF16).T)
        dv_all.append((jnp.concatenate(dv_t, axis=0) * (1.0 / SCALE)).astype(BF16).T)
    dqkv = jnp.concatenate(dq_all + dk_all + dv_all, axis=1)
    if grads:
        dqkv_ref[0] = dqkv
    da = dot(dqkv, proj_ref[:, :3 * width], ((1,), (1,)))
    back, g_gain0, g_shift0 = norm_back(h_ref[0].astype(F32), vec[0:1], da)
    dh_ref[0] = (dm + back).astype(dh_ref.dtype)
    if not grads:
        return
    total = lambda x: jnp.sum(x.astype(F32), axis=0, keepdims=True)
    small_ref[...] += jnp.concatenate(
        [g_gain0, g_gain1, g_shift0, g_shift1, total(dqkv[:, :width]), total(dqkv[:, 2 * width:]), total(dr), total(dz)], axis=0)


def attn_bwd(dc, dz, m, h, qkv, e, o, inv, proj, vec, at, parts, grads, earlier=(), after=()):
    n, seq, width = h.shape
    count = n // parts
    row = lambda *tail: pl.BlockSpec((1,) + tail, lambda i: (i + at * count,) + (0,) * len(tail))
    if grads:
        shapes = [((seq, width), F32), ((seq, width), BF16), ((seq, 3 * width), BF16)]
        specs = [row(*s) for s, _ in shapes] + [whole((8, width))]
        results = [jax.ShapeDtypeStruct((n,) + s, d) for s, d in shapes] + [jax.ShapeDtypeStruct((8, width), F32)]
    else:
        specs = [pl.BlockSpec((1, seq, width), lambda i: (i, 0, 0))]
        results = [jax.ShapeDtypeStruct((count, seq, width), BF16)]
    args = [dc, dz, m, h, qkv, e, o, inv, proj, vec]
    in_specs = [row(seq, width), row(seq, width), row(seq, width), row(seq, width), row(seq, 3 * width), row(HEADS, seq, seq),
                row(seq, width), row(seq, width), whole(proj.shape), whole(vec.shape)]
    base = len(args)
    if earlier:
        args += [earlier[3], *earlier[:3]]
        in_specs += [whole(earlier[3].shape)] + tied(3)
    aliases = {base + 1 + i: i for i in range(3)} if earlier else {}
    args += after
    in_specs += tied(len(after))
    used = len(args)

    def body(*refs):
        attn_bwd_body(grads, refs[base] if earlier else None, *refs[:base], *refs[used:])

    return pl.pallas_call(
        body,
        grid=(count,),
        in_specs=in_specs,
        out_specs=specs,
        out_shape=results,
        input_output_aliases=aliases,
        compiler_params=pltpu.CompilerParams(vmem_limit_bytes=VMEM_LIMIT),
        cost_estimate=cost(7 * count),
        name="attention_back",
    )(*args)


def proj_grad_body(a_ref, dqkv_ref, o_ref, dr_ref, small_ref, bias_ref, order_ref, keep_ref, send_ref, at_ref):
    step = pl.program_id(0)
    width = a_ref.shape[1]
    half = width // 2
    order = order_ref[...]

    def put(at, value):
        keep_ref[:, at] = value[:half].astype(BF16)
        send_ref[:, at] = value[half:].astype(BF16)

    @pl.when(step == 0)
    def _():
        at_ref[...] = dot(order, a_ref[...], ((1,), (1,))).astype(BF16)
        put(slice(3 * width, 4 * width), dot(dot(order, o_ref[...], ((1,), (1,))).astype(BF16), dr_ref[...]))
        table = jnp.concatenate([small_ref[...], bias_ref[...], jnp.zeros((112, width), F32)], axis=0).astype(BF16)
        put(slice(4 * width, None), dot(order, table, ((1,), (1,))))

    put(pl.ds(pl.multiple_of(step * width, 128), width), dot(at_ref[...], dqkv_ref[...]))


def proj_grad(a, dqkv, o, dr, small, bias, order, after=()):
    n, width = a.shape
    waits = len(after)
    shape = (width // 2, 4 * width + 128)
    return pl.pallas_call(
        lambda *refs: proj_grad_body(*refs[:7], *refs[7 + waits:]),
        grid=(3,),
        in_specs=[whole(a.shape), pl.BlockSpec((n, width), lambda i: (0, i)), whole(o.shape), whole(dr.shape), whole(small.shape), whole(bias.shape),
                  whole(order.shape)] + tied(waits),
        out_specs=[whole(shape)] * 2,
        out_shape=[jax.ShapeDtypeStruct(shape, BF16)] * 2,
        scratch_shapes=[pltpu.VMEM((width, n), BF16)],
        compiler_params=pltpu.CompilerParams(vmem_limit_bytes=VMEM_LIMIT),
        cost_estimate=cost(9),
        name="projection_gradients",
    )(a, dqkv, o, dr, small, bias, order, *after)


def place_body(count, to_ref, *refs):
    pieces, out_ref, sems = refs[:count], refs[count], refs[count + 1]
    copies = [pltpu.make_async_copy(piece, out_ref.at[to_ref[i]], sems.at[i]) for i, piece in enumerate(pieces)]
    for copy in copies:
        copy.start()
    for copy in copies:
        copy.wait()


def place(pieces, to, after=()):
    rows, columns = pieces[0].shape
    count, waits = len(pieces), len(after)
    out = pl.pallas_call(
        lambda *refs: place_body(count, *refs[:count + 1], *refs[count + 1 + waits:]),
        in_specs=[pl.BlockSpec(memory_space=pltpu.SMEM)] + [pl.BlockSpec(memory_space=pl.ANY)] * count + tied(waits),
        out_specs=pl.BlockSpec(memory_space=pltpu.VMEM),
        out_shape=jax.ShapeDtypeStruct((count, rows, columns), BF16),
        scratch_shapes=[pltpu.SemaphoreType.DMA((count,))],
        compiler_params=pltpu.CompilerParams(vmem_limit_bytes=VMEM_LIMIT),
        cost_estimate=cost(4),
        name="place_pieces",
    )(to, *pieces, *after)
    return out.reshape(count * rows, columns)


def place_down_body(count, to_ref, g_ref, m_ref, vec_ref, *refs):
    pieces, (w_ref, y_ref), (held_ref, act_ref, sems, act_sem, out_sem) = refs[:count], refs[count:count + 2], refs[count + 2:]
    rows = pieces[0].shape[0]
    copies = [pltpu.make_async_copy(piece, held_ref.at[pl.ds(pl.multiple_of(to_ref[i] * rows, rows), rows)], sems.at[i])
              for i, piece in enumerate(pieces)]
    copies.append(pltpu.make_async_copy(g_ref.at[pl.ds(0, act_ref.shape[0])], act_ref, act_sem))
    for copy in copies:
        copy.start()
    for copy in copies:
        copy.wait()
    out = pltpu.make_async_copy(held_ref, w_ref, out_sem)
    out.start()
    y_ref[...] = (m_ref[...] + vec_ref[7:8] + dot(act_ref[...], held_ref[...])).astype(BF16)
    out.wait()


def place_down(pieces, to, g, m, vec):
    rows, width = pieces[0].shape
    count = len(pieces)
    ff = count * rows
    n = g.shape[0]
    return pl.pallas_call(
        lambda *refs: place_down_body(count, *refs),
        grid=(1,),
        in_specs=[pl.BlockSpec(memory_space=pltpu.SMEM)] + tied(1) + [whole((n, width)), whole(vec.shape)] + tied(count),
        out_specs=[pl.BlockSpec(memory_space=pl.ANY), whole((n, width))],
        out_shape=[jax.ShapeDtypeStruct((ff, width), BF16), jax.ShapeDtypeStruct((n, width), BF16)],
        scratch_shapes=[pltpu.VMEM((ff, width), BF16), pltpu.VMEM((n, ff), BF16), pltpu.SemaphoreType.DMA((count,)),
                        pltpu.SemaphoreType.DMA(()), pltpu.SemaphoreType.DMA(())],
        compiler_params=pltpu.CompilerParams(vmem_limit_bytes=VMEM_LIMIT),
        cost_estimate=cost(10),
        name="place_and_feed_forward_down",
    )(to, g, m, vec, *pieces)


def finish_body(rows, per_row, width, *refs):
    *terms, down_ref, qkv_ref, out_ref, gain_ref, shift_ref, bias_ref, up_ref, wide_ref = refs
    wide_ref[0] = down_ref[...].astype(F32)
    total = terms[0][:rows].astype(F32)
    for term in terms[1:]:
        total = total + term[:rows].astype(F32)
    qkv_ref[0] = total[:, :3 * width]
    out_ref[0] = total[:, 3 * width:4 * width]
    small = total[:, 4 * width:]
    vectors = small.T
    gain_ref[0] = vectors[0:2]
    shift_ref[0] = vectors[2:4]
    bias_ref[0] = vectors[4:8]
    flat = rows * per_row
    spread = lax.broadcasted_iota(jnp.int32, (128, flat), 1) % per_row + 8 == lax.broadcasted_iota(jnp.int32, (128, flat), 0)
    wide = lax.dot_general(small, spread.astype(F32), (((1,), (0,)), ((), ())), precision=lax.Precision.HIGHEST, preferred_element_type=F32)
    here = lax.broadcasted_iota(jnp.int32, (rows, flat), 1) // per_row == lax.broadcasted_iota(jnp.int32, (rows, flat), 0)
    up_ref[...] = jnp.sum(jnp.where(here, wide, 0.0), axis=0, keepdims=True)


def finish(large, pieces, down, rows, per_row):
    columns = large[0].shape[1]
    width = (columns - 128) // 4
    shapes = [(1, rows, 3 * width), (1, rows, width), (1, 2, rows), (1, 2, rows), (1, 4, rows), (1, rows * per_row), (1, *down.shape)]
    return pl.pallas_call(
        lambda *refs: finish_body(rows, per_row, width, *refs),
        grid=(1,),
        in_specs=[pl.BlockSpec((2 * rows, columns), lambda i: (0, 0))] * len(large) + [whole(piece.shape) for piece in (*pieces, down)],
        out_specs=[whole(s) for s in shapes],
        out_shape=[jax.ShapeDtypeStruct(s, F32) for s in shapes],
        compiler_params=pltpu.CompilerParams(vmem_limit_bytes=VMEM_LIMIT),
        cost_estimate=cost(2),
        name="gather_projection_gradients",
    )(*large, *pieces, down)


def places(count):
    return count // 4, 2, 2


def hop(value, kind, step=1):
    zs, ys, cores = places(lax.axis_size("dp"))
    pairs = []
    for z in range(zs):
        for y in range(ys):
            for c in range(cores):
                to = {"core": (z, y, c ^ 1), "y": (z, y ^ 1, c), "z": ((z + step) % zs, y, c)}[kind]
                pairs.append(((z * ys + y) * cores + c, (to[0] * ys + to[1]) * cores + to[2]))
    return lax.ppermute(value, "dp", pairs)


def behind_me():
    zs, ys, cores = places(lax.axis_size("dp"))
    me = lax.axis_index("dp")
    return me // (cores * ys), (me // cores) % ys, me % cores


def along_line(shard):
    return [shard] + [hop(shard, "z", step) for step in range(1, places(lax.axis_size("dp"))[0])]


def both(mine, got):
    return (mine.astype(F32) + got.astype(F32)).astype(BF16)


def scatter_order(shard):
    zs, ys, cores = places(lax.axis_size("dp"))
    z, y, c = behind_me()
    row = jnp.arange(zs * ys * cores * shard)
    block = row // shard
    to = (((z + block % zs) % zs) * ys + (y ^ (block // zs % ys))) * cores + (c ^ (block // (zs * ys)))
    return (jnp.arange(zs * ys * cores * shard)[None, :] == (to * shard + row % shard)[:, None]).astype(BF16)


def y_step(mine, got):
    half = mine.shape[0] // 2
    return (mine[:half], got[:half]), hop(both(mine[half:], got[half:]), "y")


def z_step(mine, got):
    zs, _, _ = places(lax.axis_size("dp"))
    rows = got.shape[0] // zs
    terms = [[term[k * rows:k * rows + rows] for term in (*mine, got)] for k in range(zs)]
    return terms[0] + [hop(total(terms[k]).astype(BF16), "z", k) for k in range(1, zs)]


def total(terms):
    out = terms[0].astype(F32)
    for term in terms[1:]:
        out = out + term.astype(F32)
    return out


def held(value, *after):
    return lax.optimization_barrier((value, *after))[0]


def siblings(pieces, *after):
    return [hop(held(piece, *after), "core") for piece in pieces]


def places_of_pieces():
    zs, ys, cores = places(lax.axis_size("dp"))
    z, y, c = behind_me()
    to = []
    for core in (c, 1 - c):
        for row in (y, 1 - y):
            to += [(((z + zs - step) % zs) * ys + row) * cores + core for step in range(zs)]
    return jnp.stack(to).astype(jnp.int32)


def on_device(tokens, lengths, cotangent, w_qkv, w_out, w_up, w_down, norm_gain, norm_bias, bias_vec, up_bias):
    section = lax.axis_index("section")
    windows, seq, width = tokens.shape
    n = windows * seq
    shard = w_qkv.shape[1]
    per_row = up_bias.shape[1] // shard
    ff = w_up.shape[2]
    parts = 2
    part = windows // parts
    by_hand = lax.axis_size("dp") == 16
    table = jnp.concatenate([norm_gain[0], norm_bias[0], bias_vec[0]], axis=0).T
    table = jnp.concatenate([table, up_bias.reshape(shard, per_row)], axis=1)
    used = table.shape[1]
    table = jnp.pad(table, ((0, 0), (0, 128 - used)))
    packed = jnp.concatenate([w_qkv[0], w_out[0], table], axis=1)
    if by_hand:
        down = w_down[0]
        order, to = scatter_order(shard), places_of_pieces()
        wup = lax.all_gather(w_up[0], "dp", axis=0, tiled=True)
        proj_1, proj_3 = hop(packed, "z", 1), hop(packed, "z", 3)
        proj_y0, down_y0 = hop(packed, "y"), hop(down, "y")
        now = (proj_1, proj_3, proj_y0, order)
        proj_2, down_1 = hop(held(packed, *now), "z", 2), hop(held(down, *now), "z", 1)
        proj_y1, proj_y3 = hop(held(proj_1, *now), "y"), hop(held(proj_3, *now), "y")
        now = (proj_2, proj_y1, proj_y3, down_y0, down_1)
        down_3 = hop(held(down, *now), "z", 3)
        proj_y2, down_y1 = hop(held(proj_2, *now), "y"), hop(held(down_1, *now), "y")
        now = (down_3, proj_y2, down_y1)
        pieces = [packed, proj_1, proj_2, proj_3, proj_y0, proj_y1, proj_y2, proj_y3]
        proj = place(pieces + siblings(pieces, proj_y2), to)
        down_2 = hop(held(down, *now), "z", 2)
        down_y3 = hop(held(down_3, *now), "y")
    else:
        order = (jnp.arange(width)[None, :] == jnp.arange(width)[:, None]).astype(BF16)
        proj = lax.all_gather(packed, "dp", axis=0, tiled=True)
        wup = lax.all_gather(w_up[0], "dp", axis=0, tiled=True)
        wdown = lax.all_gather(w_down[0], "dp", axis=0, tiled=True)
    small = proj[:, 4 * width:4 * width + used]
    vec = small[:, :8].T.astype(F32)
    bup = small[:, 8:].reshape(1, ff).astype(F32)

    lengths = jnp.append(lengths, section)
    mid, c = attn_fwd(tokens, lengths, proj, False, after=(vec, bup))
    c = c.reshape(n, width)
    mid = mid.reshape(n, width)
    if by_hand:
        now = (down_2, down_y3, c)
        down_y2 = hop(held(down_2, *now), "y")
    act = mlp_up(c, wup, bup, 0, parts)
    if by_hand:
        pieces = [down, down_1, down_2, down_3, down_y0, down_y1, down_y2, down_y3]
        wdown, y_a = place_down(pieces + siblings(pieces, act), to, act, mid, vec)
    else:
        y_a, = mlp_fwd(c, mid, wup, wdown, bup, vec, False, 0, parts)
    y_b, = mlp_fwd(c, mid, wup, wdown, bup, vec, False, 1, parts, (y_a,))
    kept = ()
    arrived = [lax.ppermute(y.reshape(part, seq, width), "section", [(0, 1)]) for y in (y_a, y_b)]
    for at in range(parts):
        kept = attn_fwd(tokens, lengths, proj, True, at, parts, held(arrived[at], *kept[:1]), vec, kept)
    m, c, qkv, e, o, a, inv, h = kept
    c = c.reshape(n, width)
    y, g, gp, dc = mlp_both(c, m.reshape(n, width), cotangent.reshape(n, width), wup, wdown, bup, vec)
    dc = dc.reshape(tokens.shape)
    arrived = []
    for at in range(parts):
        back, = attn_bwd(dc, cotangent, m, h, qkv, e, o, inv, proj, vec, at, parts, False)
        arrived.append(lax.ppermute(back, "section", [(1, 0)]))
    dz = [jnp.where(section == 1, cotangent[:part], arrived[0])]
    dc, du = mlp_bwd(dz[0].reshape(part * seq, width), gp, wup, wdown, True, 0, parts)
    dz.append(jnp.where(section == 1, cotangent[part:], held(arrived[1], dc)))
    last = dz[1].reshape(part * seq, width)
    dz = jnp.concatenate(dz)
    g_down = down_grad(g, dz.reshape(n, width))
    sum_down = lax.psum_scatter(g_down, "dp", scatter_dimension=0, tiled=True)
    dc, keep_u, send_u, bup_u = mlp_grad(last, gp, wup, wdown, du, c, order, dc, (g_down,))
    dc = dc.reshape(tokens.shape)
    if by_hand:
        got_u = hop(send_u, "core")
        half = ff // 2
        rest = keep_u.shape[0] // 2
        mine_a, mine_b = [(keep_u[:rest, at], got_u[:rest, at]) for at in (slice(0, half), slice(half, ff))]
        send_a = both(keep_u[rest:, :half], got_u[rest:, :half])
        got_a = hop(send_a, "y")
        send_b = both(held(keep_u, send_a)[rest:, half:], held(got_u, send_a)[rest:, half:])
        got_b = hop(send_b, "y")
        back = attn_bwd(dc, dz, m, h, qkv, e, o, inv, proj, vec, 0, 1, True, (), (got_u,))
        terms_a = z_step(mine_a, held(got_a, back[3]))
        wait = (got_a,)
    else:
        back = attn_bwd(dc, dz, m, h, qkv, e, o, inv, proj, vec, 0, 1, True)
        wait = ()
    dh, dr, dqkv, smalls = back
    g_bup = bup_u[0].reshape(width, per_row).T
    keep_p, send_p = proj_grad(
        a.reshape(n, width), dqkv.reshape(n, 3 * width), o.reshape(n, width), dr.reshape(n, width), smalls, g_bup, order, wait)
    if by_hand:
        terms_b = z_step(mine_b, got_b)
        sum_up = jnp.concatenate([total(terms_a), total(terms_b)], axis=1)
        core_p = hop(held(send_p, got_b, *terms_a[3:]), "core")
        mine_p, got_p = y_step(keep_p, core_p)
        pieces = z_step(mine_p, held(got_p, *terms_b))[3:]
        *rest, sum_down = finish((keep_p, core_p, got_p), pieces, sum_down, shard, per_row)
    else:
        scatter = lambda *halves: lax.psum_scatter(jnp.concatenate(halves), "dp", scatter_dimension=0, tiled=True).astype(F32)
        sum_up = scatter(keep_u, send_u)
        sum_proj = scatter(keep_p, send_p)
        sum_down = sum_down[None].astype(F32)
        vectors = sum_proj[:, 4 * width:4 * width + 8].T
        rest = (
            sum_proj[None, :, :3 * width],
            sum_proj[None, :, 3 * width:4 * width],
            vectors[None, 0:2],
            vectors[None, 2:4],
            vectors[None, 4:8],
            sum_proj[:, 4 * width + 8:4 * width + used].reshape(1, -1),
        )
    return (y.reshape((1,) + tokens.shape), dh[None], rest[0], rest[1], sum_up[None], sum_down, *rest[2:])


def solution(mesh):
    sharded = [P("section", "dp", None)] * 4 + [P("section", None, "dp")] * 3 + [P("section", "dp")]
    windows = P("dp", None, None)
    out = P("section", "dp", None, None)
    return jax.shard_map(
        on_device, mesh=mesh, in_specs=(windows, P("dp"), windows, *sharded), out_specs=(out, out, *sharded), check_vma=False
    )
```

profile of v0, /device:TPU:0, one launch (start us, length us, event | category | flops | bytes accessed | tf_op | source)
XLA Modules:
  0.0 457.2 jit_solution(4778777822361414241)
XLA Ops:
  10.6 3.0 collective-permute-start.2
  13.7 3.6 collective-permute-start.1
  19.0 5.1 %collective-permute-done.1.refs_4_ = bf16[40,2688]{1,0:T(8,128)(2,1)S(1)} collective-permute-done((bf16[40,2688]{1,0:T(8,128)(2,1)S(1)}, bf16[40,2688]{1,0:T(8,128)(2,1)S(1)}, u32[]{:S(2)}, u32[]{:S(2)}) %collective-permute-start.1) | collective-permute-done | bytes 215072 | tf_op jit(solution)/shard_map/ppermute | solution.py:676
  24.1 8.3 %collective-permute-done.refs_2_ = bf16[40,2688]{1,0:T(8,128)(2,1)S(1)} collective-permute-done((bf16[40,2688]{1,0:T(8,128)(2,1)S(1)}, bf16[40,2688]{1,0:T(8,128)(2,1)S(1)}, u32[]{:S(2)}, u32[]{:S(2)}) %collective-permute-start) | collective-permute-done | bytes 215072 | tf_op jit(solution)/shard_map/ppermute | solution.py:676
  34.9 3.5 collective-permute-start.3
  40.4 17.9 %collective-permute-done.3.refs_3_ = bf16[40,2688]{1,0:T(8,128)(2,1)S(1)} collective-permute-done((bf16[40,2688]{1,0:T(8,128)(2,1)S(1)}, bf16[40,2688]{1,0:T(8,128)(2,1)S(1)}, u32[]{:S(2)}, u32[]{:S(2)}) %collective-permute-start.3) | collective-permute-done | bytes 215072 | tf_op jit(solution)/shard_map/ppermute | solution.py:676
  62.0 8.8 %collective-permute-done.8.refs_7_ = bf16[40,2688]{1,0:T(8,128)(2,1)} collective-permute-done((bf16[40,2688]{1,0:T(8,128)(2,1)S(1)}, bf16[40,2688]{1,0:T(8,128)(2,1)}, u32[]{:S(2)}, u32[]{:S(2)}) %collective-permute-start.8) | collective-permute-done | bytes 215072 | tf_op jit(solution)/shard_map/ppermute | solution.py:676
  71.3 12.7 %collective-permute-done.17.refs_7_ = bf16[320,640]{1,0:T(8,128)(2,1)S(1)} collective-permute-done((bf16[320,640]{1,0:T(8,128)(2,1)S(1)}, bf16[320,640]{1,0:T(8,128)(2,1)S(1)}, u32[]{:S(2)}, u32[]{:S(2)}) %collective-permute-start.17) | collective-permute-done | bytes 409632 | tf_op jit(solution)/shard_map/ppermute | solution.py:676
  91.4 4.8 %place_pieces.1 = bf16[16,40,2688]{2,1,0:T(8,128)(2,1)} custom-call(s32[16]{0:T(128)} %stack.67.refs_0_, bf16[40,2688]{1,0:T(8,128)(2,1)} %copy-done.8, bf16[40,2688]{1,0:T(8,128)(2,1)} %copy-done.27, bf16[40,2688]{1,0:T(8,128)(2,1)} %copy-done.28, bf16[40,2688]{1,0:T(8,128)(2,1)} %copy-done.26, bf16[40,2688]{1,0:T(8,128)(2,1)} %copy-done.25, ...), custom_call_target="tpu_custom_call" | custom-call | flops 4400000000 | bytes 1024 | tf_op jit(solution)/shard_map/place_pieces/pallas_call | solution.py:580
  98.9 16.7 %attention_forward.3 = (f32[4,256,640]{2,1,0:T(8,128)}, bf16[4,256,640]{2,1,0:T(8,128)(2,1)}) custom-call(s32[5]{0:T(128)} %pad_add_fusion.refs_0_, bf16[4,256,640]{2,1,0:T(8,128)(2,1)} %refs_1_.7, bf16[640,2688]{1,0:T(8,128)(2,1)} %bitcast.57, f32[8,640]{1,0:T(8,128)} %convert_bitcast_fusion.refs_3_.refs_5_.refs_4_.refs_6_.refs_9_, ...), custom_call_target="tpu_custom_call" | custom-call | flops 19800000512 | bytes 1024 | tf_op jit(solution)/shard_map/attention_forward/pallas_call | solution.py:131
  119.0 8.6 %feed_forward_up.1.refs_1_ = bf16[512,5120]{1,0:T(8,128)(2,1)} custom-call(bf16[1024,640]{1,0:T(8,128)(2,1)} %bitcast.89, bf16[640,5120]{1,0:T(8,128)(2,1)} %bitcast.67, f32[1,5120]{1,0:T(1,128)} %reshape.200.refs_4_.refs_2_.refs_5_), custom_call_target="tpu_custom_call" | custom-call | flops 7040000000 | bytes 1024 | tf_op jit(solution)/shard_map/feed_forward_up/pallas_call | solution.py:252
  134.2 11.0 %place_and_feed_forward_down.1 = (bf16[5120,640]{1,0:T(8,128)(2,1)}, bf16[512,640]{1,0:T(8,128)(2,1)}) custom-call(s32[16]{0:T(128)} %stack.67.refs_0_, bf16[512,5120]{1,0:T(8,128)(2,1)} %feed_forward_up.1.refs_1_, f32[1024,640]{1,0:T(8,128)} %bitcast.82, f32[8,640]{1,0:T(8,128)} %convert_bitcast_fusion.refs_3_.refs_5_.refs_4_.refs_6_.refs_9_, ...), custom_call_target="tpu_custom_call" | custom-call | flops 11000000512 | bytes 1024 | tf_op jit(solution)/shard_map/place_and_feed_forward_down/pallas_call | solution.py:614
  145.2 3.6 collective-permute-start.31
  148.9 13.2 %feed_forward.1 = bf16[512,640]{1,0:T(8,128)(2,1)} custom-call(bf16[1024,640]{1,0:T(8,128)(2,1)} %bitcast.90, f32[1024,640]{1,0:T(8,128)} %bitcast.83, bf16[640,5120]{1,0:T(8,128)(2,1)} %bitcast.68, bf16[5120,640]{1,0:T(8,128)(2,1)} %get-tuple-element.114.refs_3_.refs_4_, f32[1,5120]{1,0:T(1,128)} %reshape.200.refs_4_.refs_2_.refs_5_, ...), custom_call_target="tpu_custom_call" | custom-call | flops 28600000512 | bytes 1024 | tf_op jit(solution)/shard_map/feed_forward/pallas_call | solution.py:184
  164.2 11.7 %attention_forward.4 = (f32[4,256,640]{2,1,0:T(8,128)}, bf16[4,256,640]{2,1,0:T(8,128)(2,1)}, bf16[4,256,1920]{2,1,0:T(8,128)(2,1)}, bf16[4,20,256,256]{3,2,1,0:...) custom-call(s32[5]{0:T(128)} %pad_add_fusion.refs_0_, ...), custom_call_target="tpu_custom_call" | custom-call | flops 9900000256 | bytes 1024 | tf_op jit(solution)/shard_map/attention_forward/pallas_call | solution.py:131
  178.8 11.7 %attention_forward.5 = (f32[4,256,640]{2,1,0:T(8,128)}, bf16[4,256,640]{2,1,0:T(8,128)(2,1)}, bf16[4,256,1920]{2,1,0:T(8,128)(2,1)}, bf16[4,20,256,256]{3,2,1,0:...) custom-call(s32[5]{0:T(128)} %pad_add_fusion.refs_0_, ...), custom_call_target="tpu_custom_call", output_to_operand_aliasing={{0}: (5, {}), {1}: (6, {}), {2}: (7, {}), {3}: (8, {}), {4}... | custom-call | flops 9900000256 | bytes 1024 | tf_op jit(solution)/shard_map/attention_forward/pallas_call | solution.py:131
  190.4 43.8 %feed_forward_both.1 = (bf16[1024,640]{1,0:T(8,128)(2,1)}, bf16[1024,5120]{1,0:T(8,128)(2,1)}, bf16[1024,5120]{1,0:T(8,128)(2,1)}, f32[1024,640]{1,0:T(8,128)}) custom-call(bf16[1024,640]{1,0:T(8,128)(2,1)} %bitcast.92, f32[1024,640]{1,0:T(8,128)} %bitcast.84, bf16[1024,640]{1,0:T(8,128)(2,1)} %bitcast.51, bf16[640,5120]{1,0:T(8,128)(2,1)} %bitcast.69, ...), custom_call_target="tpu_custom_call" | custom-call | flops 46200000512 | bytes 1024 | tf_op jit(solution)/shard_map/feed_forward_both/pallas_call | solution.py:226
  234.3 14.9 %attention_back.4 = bf16[2,256,640]{2,1,0:T(8,128)(2,1)} custom-call(f32[4,256,640]{2,1,0:T(8,128)} %bitcast.86, bf16[4,256,640]{2,1,0:T(8,128)(2,1)} %refs_1_.9, f32[4,256,640]{2,1,0:T(8,128)} %get-tuple-element.126.refs_2_, bf16[4,256,640]{2,1,0:T(8,128)(2,1)} %get-tuple-element.129.refs_3_, bf16[4,256,1920]{2,1,0:T(8,128)(2,1)} %get-tuple-element.130.refs_4_, ...), custom_call_target="tpu_custom_call" | custom-call | flops 15399999488 | bytes 1024 | tf_op jit(solution)/shard_map/attention_back/pallas_call | solution.py:517
  250.6 14.7 %attention_back.3 = bf16[2,256,640]{2,1,0:T(8,128)(2,1)} custom-call(f32[4,256,640]{2,1,0:T(8,128)} %bitcast.87, bf16[4,256,640]{2,1,0:T(8,128)(2,1)} %refs_1_.9, f32[4,256,640]{2,1,0:T(8,128)} %get-tuple-element.126.refs_2_, bf16[4,256,640]{2,1,0:T(8,128)(2,1)} %get-tuple-element.129.refs_3_, bf16[4,256,1920]{2,1,0:T(8,128)(2,1)} %get-tuple-element.130.refs_4_, ...), custom_call_target="tpu_custom_call" | custom-call | flops 15399999488 | bytes 1024 | tf_op jit(solution)/shard_map/attention_back/pallas_call | solution.py:517
  268.3 13.5 %feed_forward_back.1 = (f32[1024,640]{1,0:T(8,128)}, bf16[512,5120]{1,0:T(8,128)(2,1)}) custom-call(bf16[512,640]{1,0:T(8,128)(2,1)} %bitcast.50, bf16[1024,5120]{1,0:T(8,128)(2,1)} %get-tuple-element.134.refs_1_, bf16[640,5120]{1,0:T(8,128)(2,1)} %bitcast.70, bf16[5120,640]{1,0:T(8,128)(2,1)} %get-tuple-element.114.refs_3_.refs_4_), custom_call_target="tpu_custom_call" | custom-call | flops 12099999744 | bytes 1024 | tf_op jit(solution)/shard_map/feed_forward_back/pallas_call | solution.py:319
  284.9 12.4 %down_gradient.1.refs_8_ = bf16[5120,640]{1,0:T(8,128)(2,1)} custom-call(bf16[1024,5120]{1,0:T(8,128)(2,1)} %get-tuple-element.138.refs_0_, bf16[1024,640]{1,0:T(8,128)(2,1)} %bitcast.52), custom_call_target="tpu_custom_call" | custom-call | flops 13200000000 | bytes 1024 | tf_op jit(solution)/shard_map/down_gradient/pallas_call | solution.py:417
  297.3 22.5 %feed_forward_gradients.1 = (f32[1024,640]{1,0:T(8,128)}, bf16[320,5120]{1,0:T(8,128)(2,1)}, bf16[320,5120]{1,0:T(8,128)(2,1)}, f32[8,5120]{1,0:T(8,128)}) custom-call(bf16[512,640]{1,0:T(8,128)(2,1)} %bitcast.49, bf16[1024,5120]{1,0:T(8,128)(2,1)} %get-tuple-element.134.refs_1_, bf16[640,5120]{1,0:T(8,128)(2,1)} %bitcast.71, ...), custom_call_target="tpu_custom_call", output_to_operand_aliasing={{0}: (7, {})} | custom-call | flops 23100000256 | bytes 1024 | tf_op jit(solution)/shard_map/feed_forward_gradients/pallas_call | solution.py:394
  330.9 25.5 %attention_back.5 = (f32[4,256,640]{2,1,0:T(8,128)}, bf16[4,256,640]{2,1,0:T(8,128)(2,1)}, bf16[4,256,1920]{2,1,0:T(8,128)(2,1)}, f32[8,640]{1,0:T(8,128)}) custom-call(f32[4,256,640]{2,1,0:T(8,128)} %bitcast.85, bf16[4,256,640]{2,1,0:T(8,128)(2,1)} %pad_maximum_fusion.refs_1_, f32[4,256,640]{2,1,0:T(8,128)} %get-tuple-element.126.refs_2_, ...), custom_call_target="tpu_custom_call" | custom-call | flops 30799998976 | bytes 1024 | tf_op jit(solution)/shard_map/attention_back/pallas_call | solution.py:517
  360.9 11.7 %projection_gradients.1 = (bf16[320,2688]{1,0:T(8,128)(2,1)}, bf16[320,2688]{1,0:T(8,128)(2,1)}) custom-call(bf16[1024,640]{1,0:T(8,128)(2,1)} %bitcast.95, bf16[1024,1920]{1,0:T(8,128)(2,1)} %bitcast.80, bf16[1024,640]{1,0:T(8,128)(2,1)} %bitcast.94, bf16[1024,640]{1,0:T(8,128)(2,1)} %bitcast.91, f32[8,640]{1,0:T(8,128)} %get-tuple-element.145.refs_4_, ...), custom_call_target="tpu_custom_call" | custom-call | flops 9900000256 | bytes 1024 | tf_op jit(solution)/shard_map/projection_gradients/pallas_call | solution.py:554
  372.6 7.3 %collective-permute-done.36 = bf16[160,2560]{1,0:T(8,128)(2,1)S(1)} collective-permute-done((bf16[160,2560]{1,0:T(8,128)(2,1)S(1)}, bf16[160,2560]{1,0:T(8,128)(2,1)S(1)}, u32[]{:S(2)}, u32[]{:S(2)}) %collective-permute-start.36) | collective-permute-done | bytes 819232 | tf_op jit(solution)/shard_map/ppermute | solution.py:676
  379.9 6.3 %collective-permute-done.38 = bf16[40,2560]{1,0:T(8,128)(2,1)S(1)} collective-permute-done((bf16[40,2560]{1,0:T(8,128)(2,1)S(1)}, bf16[40,2560]{1,0:T(8,128)(2,1)S(1)}, u32[]{:S(2)}, u32[]{:S(2)}) %collective-permute-start.38) | collective-permute-done | bytes 204832 | tf_op jit(solution)/shard_map/ppermute | solution.py:676
  388.0 4.7 %collective-permute-start.43 = (bf16[40,2560]{1,0:T(8,128)(2,1)S(1)}, bf16[40,2560]{1,0:T(8,128)(2,1)S(1)}, u32[]{:S(2)}, u32[]{:S(2)}) collective-permute-start(bf16[40,2560]{1,0:T(8,128)(2,1)S(1)} %get-tuple-element.163), channel_id=1, source_target_pairs={{0,8},{1,9},{2,10},{3,11},{4,12},{5,13},{6,14},{7,15},{8,0},{9,1},... | collective-permute-start | bytes 614408 | tf_op jit(solution)/shard_map/ppermute | solution.py:676
  395.6 5.1 %collective-permute-done.44 = bf16[40,2560]{1,0:T(8,128)(2,1)S(1)} collective-permute-done((bf16[40,2560]{1,0:T(8,128)(2,1)S(1)}, bf16[40,2560]{1,0:T(8,128)(2,1)S(1)}, u32[]{:S(2)}, u32[]{:S(2)}) %collective-permute-start.44) | collective-permute-done | bytes 204832 | tf_op jit(solution)/shard_map/ppermute | solution.py:676
  400.7 13.3 %collective-permute-done.43 = bf16[40,2560]{1,0:T(8,128)(2,1)S(1)} collective-permute-done((bf16[40,2560]{1,0:T(8,128)(2,1)S(1)}, bf16[40,2560]{1,0:T(8,128)(2,1)S(1)}, u32[]{:S(2)}, u32[]{:S(2)}) %collective-permute-start.43) | collective-permute-done | bytes 204832 | tf_op jit(solution)/shard_map/ppermute | solution.py:676
  415.1 3.9 collective-permute-done.41.refs_2_
  422.3 9.1 %collective-permute-done.47.refs_5_ = bf16[40,2688]{1,0:T(8,128)(2,1)S(1)} collective-permute-done((bf16[40,2688]{1,0:T(8,128)(2,1)S(1)}, bf16[40,2688]{1,0:T(8,128)(2,1)S(1)}, u32[]{:S(2)}, u32[]{:S(2)}) %collective-permute-start.47) | collective-permute-done | bytes 215072 | tf_op jit(solution)/shard_map/ppermute | solution.py:676
  431.3 14.8 %collective-permute-done.46.refs_4_ = bf16[40,2688]{1,0:T(8,128)(2,1)S(1)} collective-permute-done((bf16[40,2688]{1,0:T(8,128)(2,1)S(1)}, bf16[40,2688]{1,0:T(8,128)(2,1)S(1)}, u32[]{:S(2)}, u32[]{:S(2)}) %collective-permute-start.46) | collective-permute-done | bytes 215072 | tf_op jit(solution)/shard_map/ppermute | solution.py:676
  (188 shorter events, 74.6 us)
Async XLA Ops:
  7.2 111.8 %all-gather.3.cloned.1.call-start = ((), (), s32[]{:S(2)}) async-start(), calls=%async_computation.2 | async-start | bytes 6963200 | tf_op jit(solution)/shard_map/all_gather | solution.py:757
  7.9 438.2 %reduce-scatter.2.cloned.1.call-start = ((), (), s32[]{:S(2)}) async-start(), calls=%async_computation.1 | async-start | bytes 6963200 | tf_op jit(solution)/shard_map/reduce_scatter | solution.py:812
  17.3 15.1 %collective-permute-start = (bf16[40,2688]{1,0:T(8,128)(2,1)S(1)}, bf16[40,2688]{1,0:T(8,128)(2,1)S(1)}, u32[]{:S(2)}, u32[]{:S(2)}) collective-permute-start(bf16[40,2688]{1,0:T(8,128)(2,1)S(1)} %pad_maximum_fusion.1.refs_1_), channel_id=1, source_target_pairs={{0,4},{1,5},{2,6},{3,7},{4,8},{5,9},{6,10},{7,11},{8,12},{9,13},{1... | collective-permute-start | bytes 645128 | tf_op jit(solution)/shard_map/ppermute | solution.py:676
  17.3 23.1 %collective-permute-start.6 = (bf16[320,640]{1,0:T(8,128)(2,1)}, bf16[320,640]{1,0:T(8,128)(2,1)S(1)}, u32[]{:S(2)}, u32[]{:S(2)}) collective-permute-start(bf16[320,640]{1,0:T(8,128)(2,1)} %bitcast.74), channel_id=1, source_target_pairs={{0,2},{1,3},{2,0},{3,1},{4,6},{5,7},{6,4},{7,5},{8,10},{9,11},{10,... | collective-permute-start | bytes 1228808 | tf_op jit(solution)/shard_map/ppermute | solution.py:676
  32.4 25.9 %collective-permute-start.7 = (bf16[320,640]{1,0:T(8,128)(2,1)S(1)}, bf16[320,640]{1,0:T(8,128)(2,1)S(1)}, u32[]{:S(2)}, u32[]{:S(2)}) collective-permute-start(bf16[320,640]{1,0:T(8,128)(2,1)S(1)} %bitcast.76), channel_id=1, source_target_pairs={{0,4},{1,5},{2,6},{3,7},{4,8},{5,9},{6,10},{7,11},{8,12},{9,13},{1... | collective-permute-start | bytes 1228808 | tf_op jit(solution)/shard_map/ppermute | solution.py:676
  34.9 23.4 %collective-permute-start.3 = (bf16[40,2688]{1,0:T(8,128)(2,1)S(1)}, bf16[40,2688]{1,0:T(8,128)(2,1)S(1)}, u32[]{:S(2)}, u32[]{:S(2)}) collective-permute-start(bf16[40,2688]{1,0:T(8,128)(2,1)S(1)} %pad_maximum_fusion.1.refs_1_), channel_id=1, source_target_pairs={{0,8},{1,9},{2,10},{3,11},{4,12},{5,13},{6,14},{7,15},{8,0},{9,1},... | collective-permute-start | bytes 645128 | tf_op jit(solution)/shard_map/ppermute | solution.py:676
  38.3 19.9 %collective-permute-start.4 = (bf16[40,2688]{1,0:T(8,128)(2,1)S(1)}, bf16[40,2688]{1,0:T(8,128)(2,1)}, u32[]{:S(2)}, u32[]{:S(2)}) collective-permute-start(bf16[40,2688]{1,0:T(8,128)(2,1)S(1)} %collective-permute-done.refs_2_), channel_id=1, source_target_pairs={{0,2},{1,3},{2,0},{3,1},{4,6},{5,7},{6,4},{7,5},{8,10},{9,11},{10,... | collective-permute-start | bytes 645128 | tf_op jit(solution)/shard_map/ppermute | solution.py:676
  38.3 19.9 %collective-permute-start.5 = (bf16[40,2688]{1,0:T(8,128)(2,1)S(1)}, bf16[40,2688]{1,0:T(8,128)(2,1)}, u32[]{:S(2)}, u32[]{:S(2)}) collective-permute-start(bf16[40,2688]{1,0:T(8,128)(2,1)S(1)} %collective-permute-done.1.refs_4_), channel_id=1, source_target_pairs={{0,2},{1,3},{2,0},{3,1},{4,6},{5,7},{6,4},{7,5},{8,10},{9,11},{10,... | collective-permute-start | bytes 645128 | tf_op jit(solution)/shard_map/ppermute | solution.py:676
  58.3 12.4 %collective-permute-start.8 = (bf16[40,2688]{1,0:T(8,128)(2,1)S(1)}, bf16[40,2688]{1,0:T(8,128)(2,1)}, u32[]{:S(2)}, u32[]{:S(2)}) collective-permute-start(bf16[40,2688]{1,0:T(8,128)(2,1)S(1)} %collective-permute-done.3.refs_3_), channel_id=1, source_target_pairs={{0,2},{1,3},{2,0},{3,1},{4,6},{5,7},{6,4},{7,5},{8,10},{9,11},{10,... | collective-permute-start | bytes 645128 | tf_op jit(solution)/shard_map/ppermute | solution.py:676
  58.9 25.1 %collective-permute-start.17 = (bf16[320,640]{1,0:T(8,128)(2,1)S(1)}, bf16[320,640]{1,0:T(8,128)(2,1)S(1)}, u32[]{:S(2)}, u32[]{:S(2)}) collective-permute-start(bf16[320,640]{1,0:T(8,128)(2,1)S(1)} %bitcast.77), channel_id=1, source_target_pairs={{0,12},{1,13},{2,14},{3,15},{4,0},{5,1},{6,2},{7,3},{8,4},{9,5},{1... | collective-permute-start | bytes 1228808 | tf_op jit(solution)/shard_map/ppermute | solution.py:676
  60.5 26.1 %collective-permute-start.18 = (bf16[320,640]{1,0:T(8,128)(2,1)S(1)}, bf16[320,640]{1,0:T(8,128)(2,1)S(1)}, u32[]{:S(2)}, u32[]{:S(2)}) collective-permute-start(bf16[320,640]{1,0:T(8,128)(2,1)S(1)} %collective-permute-done.7.refs_5_), channel_id=1, source_target_pairs={{0,2},{1,3},{2,0},{3,1},{4,6},{5,7},{6,4},{7,5},{8,10},{9,11},{10,... | collective-permute-start | bytes 1228808 | tf_op jit(solution)/shard_map/ppermute | solution.py:676
  70.7 15.8 %collective-permute-start.9 = (bf16[40,2688]{1,0:T(8,128)(2,1)S(1)}, bf16[40,2688]{1,0:T(8,128)(2,1)S(1)}, u32[]{:S(2)}, u32[]{:S(2)}) collective-permute-start(bf16[40,2688]{1,0:T(8,128)(2,1)S(1)} %pad_maximum_fusion.1.refs_1_), channel_id=1, source_target_pairs={{0,1},{1,0},{2,3},{3,2},{4,5},{5,4},{6,7},{7,6},{8,9},{9,8},{10,11... | collective-permute-start | bytes 645128 | tf_op jit(solution)/shard_map/ppermute | solution.py:676
  70.7 16.3 %collective-permute-start.10 = (bf16[40,2688]{1,0:T(8,128)(2,1)S(1)}, bf16[40,2688]{1,0:T(8,128)(2,1)S(1)}, u32[]{:S(2)}, u32[]{:S(2)}) collective-permute-start(bf16[40,2688]{1,0:T(8,128)(2,1)S(1)} %collective-permute-done.refs_2_), channel_id=1, source_target_pairs={{0,1},{1,0},{2,3},{3,2},{4,5},{5,4},{6,7},{7,6},{8,9},{9,8},{10,11... | collective-permute-start | bytes 645128 | tf_op jit(solution)/shard_map/ppermute | solution.py:676
  71.3 16.0 %collective-permute-start.11 = (bf16[40,2688]{1,0:T(8,128)(2,1)S(1)}, bf16[40,2688]{1,0:T(8,128)(2,1)S(1)}, u32[]{:S(2)}, u32[]{:S(2)}) collective-permute-start(bf16[40,2688]{1,0:T(8,128)(2,1)S(1)} %collective-permute-done.3.refs_3_), channel_id=1, source_target_pairs={{0,1},{1,0},{2,3},{3,2},{4,5},{5,4},{6,7},{7,6},{8,9},{9,8},{10,11... | collective-permute-start | bytes 645128 | tf_op jit(solution)/shard_map/ppermute | solution.py:676
  89.8 27.1 %collective-permute-start.19 = (bf16[320,640]{1,0:T(8,128)(2,1)S(1)}, bf16[320,640]{1,0:T(8,128)(2,1)S(1)}, u32[]{:S(2)}, u32[]{:S(2)}) collective-permute-start(bf16[320,640]{1,0:T(8,128)(2,1)S(1)} %bitcast.78), channel_id=1, source_target_pairs={{0,8},{1,9},{2,10},{3,11},{4,12},{5,13},{6,14},{7,15},{8,0},{9,1},... | collective-permute-start | bytes 1228808 | tf_op jit(solution)/shard_map/ppermute | solution.py:676
  90.5 26.4 %collective-permute-start.20 = (bf16[320,640]{1,0:T(8,128)(2,1)S(1)}, bf16[320,640]{1,0:T(8,128)(2,1)S(1)}, u32[]{:S(2)}, u32[]{:S(2)}) collective-permute-start(bf16[320,640]{1,0:T(8,128)(2,1)S(1)} %collective-permute-done.17.refs_7_), channel_id=1, source_target_pairs={{0,2},{1,3},{2,0},{3,1},{4,6},{5,7},{6,4},{7,5},{8,10},{9,11},{10,... | collective-permute-start | bytes 1228808 | tf_op jit(solution)/shard_map/ppermute | solution.py:676
  145.2 18.2 %collective-permute-start.31 = (bf16[2,256,640]{2,1,0:T(8,128)(2,1)}, bf16[2,256,640]{2,1,0:T(8,128)(2,1)S(1)}, u32[]{:S(2)}, u32[]{:S(2)}) collective-permute-start(bf16[2,256,640]{2,1,0:T(8,128)(2,1)} %bitcast.72), channel_id=1, source_target_pairs={{0,16},{1,17},{2,18},{3,19},{4,20},{5,21},{6,22},{7,23},{8,24},{9,... | collective-permute-start | bytes 1966088 | tf_op jit(solution)/shard_map/ppermute | solution.py:795
  162.1 15.9 %collective-permute-start.30 = (bf16[2,256,640]{2,1,0:T(8,128)(2,1)}, bf16[2,256,640]{2,1,0:T(8,128)(2,1)S(1)}, u32[]{:S(2)}, u32[]{:S(2)}) collective-permute-start(bf16[2,256,640]{2,1,0:T(8,128)(2,1)} %bitcast.73), channel_id=1, source_target_pairs={{0,16},{1,17},{2,18},{3,19},{4,20},{5,21},{6,22},{7,23},{8,24},{9,... | collective-permute-start | bytes 1966088 | tf_op jit(solution)/shard_map/ppermute | solution.py:795
  249.2 18.2 %collective-permute-start.33 = (bf16[2,256,640]{2,1,0:T(8,128)(2,1)}, bf16[2,256,640]{2,1,0:T(8,128)(2,1)S(1)}, u32[]{:S(2)}, u32[]{:S(2)}) collective-permute-start(bf16[2,256,640]{2,1,0:T(8,128)(2,1)} %attention_back.4), channel_id=1, source_target_pairs={{16,0},{17,1},{18,2},{19,3},{20,4},{21,5},{22,6},{23,7},{24,8},{25... | collective-permute-start | bytes 1966088 | tf_op jit(solution)/shard_map/ppermute | solution.py:805
  265.4 18.1 %collective-permute-start.32 = (bf16[2,256,640]{2,1,0:T(8,128)(2,1)}, bf16[2,256,640]{2,1,0:T(8,128)(2,1)S(1)}, u32[]{:S(2)}, u32[]{:S(2)}) collective-permute-start(bf16[2,256,640]{2,1,0:T(8,128)(2,1)} %attention_back.3), channel_id=1, source_target_pairs={{16,0},{17,1},{18,2},{19,3},{20,4},{21,5},{22,6},{23,7},{24,8},{25... | collective-permute-start | bytes 1966088 | tf_op jit(solution)/shard_map/ppermute | solution.py:805
  327.4 29.1 %collective-permute-start.35 = (bf16[160,2560]{1,0:T(8,128)(2,1)S(1)}, bf16[160,2560]{1,0:T(8,128)(2,1)S(1)}, u32[]{:S(2)}, u32[]{:S(2)}) collective-permute-start(bf16[160,2560]{1,0:T(8,128)(2,1)S(1)} %add_convert_fusion.2), channel_id=1, source_target_pairs={{0,2},{1,3},{2,0},{3,1},{4,6},{5,7},{6,4},{7,5},{8,10},{9,11},{10,... | collective-permute-start | bytes 2457608 | tf_op jit(solution)/shard_map/ppermute | solution.py:676
  330.3 49.6 %collective-permute-start.36 = (bf16[160,2560]{1,0:T(8,128)(2,1)S(1)}, bf16[160,2560]{1,0:T(8,128)(2,1)S(1)}, u32[]{:S(2)}, u32[]{:S(2)}) collective-permute-start(bf16[160,2560]{1,0:T(8,128)(2,1)S(1)} %add_convert_fusion.1), channel_id=1, source_target_pairs={{0,2},{1,3},{2,0},{3,1},{4,6},{5,7},{6,4},{7,5},{8,10},{9,11},{10,... | collective-permute-start | bytes 2457608 | tf_op jit(solution)/shard_map/ppermute | solution.py:676
  358.1 21.7 %collective-permute-start.39 = (bf16[40,2560]{1,0:T(8,128)(2,1)S(1)}, bf16[40,2560]{1,0:T(8,128)(2,1)S(1)}, u32[]{:S(2)}, u32[]{:S(2)}) collective-permute-start(bf16[40,2560]{1,0:T(8,128)(2,1)S(1)} %get-tuple-element.165), channel_id=1, source_target_pairs={{0,12},{1,13},{2,14},{3,15},{4,0},{5,1},{6,2},{7,3},{8,4},{9,5},{1... | collective-permute-start | bytes 614408 | tf_op jit(solution)/shard_map/ppermute | solution.py:676
  360.2 25.9 %collective-permute-start.38 = (bf16[40,2560]{1,0:T(8,128)(2,1)S(1)}, bf16[40,2560]{1,0:T(8,128)(2,1)S(1)}, u32[]{:S(2)}, u32[]{:S(2)}) collective-permute-start(bf16[40,2560]{1,0:T(8,128)(2,1)S(1)} %get-tuple-element.166), channel_id=1, source_target_pairs={{0,8},{1,9},{2,10},{3,11},{4,12},{5,13},{6,14},{7,15},{8,0},{9,1},... | collective-permute-start | bytes 614408 | tf_op jit(solution)/shard_map/ppermute | solution.py:676
  360.2 25.9 %collective-permute-start.37 = (bf16[40,2560]{1,0:T(8,128)(2,1)S(1)}, bf16[40,2560]{1,0:T(8,128)(2,1)S(1)}, u32[]{:S(2)}, u32[]{:S(2)}) collective-permute-start(bf16[40,2560]{1,0:T(8,128)(2,1)S(1)} %get-tuple-element.167), channel_id=1, source_target_pairs={{0,4},{1,5},{2,6},{3,7},{4,8},{5,9},{6,10},{7,11},{8,12},{9,13},{1... | collective-permute-start | bytes 614408 | tf_op jit(solution)/shard_map/ppermute | solution.py:676
  388.0 12.7 %collective-permute-start.44 = (bf16[40,2560]{1,0:T(8,128)(2,1)S(1)}, bf16[40,2560]{1,0:T(8,128)(2,1)S(1)}, u32[]{:S(2)}, u32[]{:S(2)}) collective-permute-start(bf16[40,2560]{1,0:T(8,128)(2,1)S(1)} %get-tuple-element.162), channel_id=1, source_target_pairs={{0,12},{1,13},{2,14},{3,15},{4,0},{5,1},{6,2},{7,3},{8,4},{9,5},{1... | collective-permute-start | bytes 614408 | tf_op jit(solution)/shard_map/ppermute | solution.py:676
  388.0 25.9 %collective-permute-start.43 = (bf16[40,2560]{1,0:T(8,128)(2,1)S(1)}, bf16[40,2560]{1,0:T(8,128)(2,1)S(1)}, u32[]{:S(2)}, u32[]{:S(2)}) collective-permute-start(bf16[40,2560]{1,0:T(8,128)(2,1)S(1)} %get-tuple-element.163), channel_id=1, source_target_pairs={{0,8},{1,9},{2,10},{3,11},{4,12},{5,13},{6,14},{7,15},{8,0},{9,1},... | collective-permute-start | bytes 614408 | tf_op jit(solution)/shard_map/ppermute | solution.py:676
  392.7 21.2 %collective-permute-start.42 = (bf16[40,2560]{1,0:T(8,128)(2,1)S(1)}, bf16[40,2560]{1,0:T(8,128)(2,1)S(1)}, u32[]{:S(2)}, u32[]{:S(2)}) collective-permute-start(bf16[40,2560]{1,0:T(8,128)(2,1)S(1)} %get-tuple-element.164), channel_id=1, source_target_pairs={{0,4},{1,5},{2,6},{3,7},{4,8},{5,9},{6,10},{7,11},{8,12},{9,13},{1... | collective-permute-start | bytes 614408 | tf_op jit(solution)/shard_map/ppermute | solution.py:676
  394.9 24.1 %collective-permute-start.41 = (bf16[160,2688]{1,0:T(8,128)(2,1)S(1)}, bf16[160,2688]{1,0:T(8,128)(2,1)S(1)}, u32[]{:S(2)}, u32[]{:S(2)}) collective-permute-start(bf16[160,2688]{1,0:T(8,128)(2,1)S(1)} %add_convert_fusion), channel_id=1, source_target_pairs={{0,2},{1,3},{2,0},{3,1},{4,6},{5,7},{6,4},{7,5},{8,10},{9,11},{10,... | collective-permute-start | bytes 2580488 | tf_op jit(solution)/shard_map/ppermute | solution.py:676
  419.2 12.1 %collective-permute-start.47 = (bf16[40,2688]{1,0:T(8,128)(2,1)S(1)}, bf16[40,2688]{1,0:T(8,128)(2,1)S(1)}, u32[]{:S(2)}, u32[]{:S(2)}) collective-permute-start(bf16[40,2688]{1,0:T(8,128)(2,1)S(1)} %get-tuple-element.169), channel_id=1, source_target_pairs={{0,12},{1,13},{2,14},{3,15},{4,0},{5,1},{6,2},{7,3},{8,4},{9,5},{1... | collective-permute-start | bytes 645128 | tf_op jit(solution)/shard_map/ppermute | solution.py:676
  419.8 26.4 %collective-permute-start.46 = (bf16[40,2688]{1,0:T(8,128)(2,1)S(1)}, bf16[40,2688]{1,0:T(8,128)(2,1)S(1)}, u32[]{:S(2)}, u32[]{:S(2)}) collective-permute-start(bf16[40,2688]{1,0:T(8,128)(2,1)S(1)} %get-tuple-element.170), channel_id=1, source_target_pairs={{0,8},{1,9},{2,10},{3,11},{4,12},{5,13},{6,14},{7,15},{8,0},{9,1},... | collective-permute-start | bytes 645128 | tf_op jit(solution)/shard_map/ppermute | solution.py:676
  419.8 26.4 %collective-permute-start.45 = (bf16[40,2688]{1,0:T(8,128)(2,1)S(1)}, bf16[40,2688]{1,0:T(8,128)(2,1)S(1)}, u32[]{:S(2)}, u32[]{:S(2)}) collective-permute-start(bf16[40,2688]{1,0:T(8,128)(2,1)S(1)} %get-tuple-element.171), channel_id=1, source_target_pairs={{0,4},{1,5},{2,6},{3,7},{4,8},{5,9},{6,10},{7,11},{8,12},{9,13},{1... | collective-permute-start | bytes 645128 | tf_op jit(solution)/shard_map/ppermute | solution.py:676
  (55 other events, 881.3 us)
Sparse Core Ops, SparseCore 0:
  10.3 104.0 all-gather.2
  320.0 116.2 reduce-scatter.1
where the time goes:
time: 466 us; the launch traced here: 457 us
  Pallas kernels  240 us (52%)
  waiting for transfers between devices  127 us (27%)
  starting transfers between devices  46.7 us (10%)
  other arithmetic  16.9 us (4%)
  between operations  14.9 us (3%)
  local copies, waits for them, and re-layouts  11.5 us (2%)
    ppermute x44, waiting for transfers between devices, hop(): return lax.ppermute(value, 'dp', pairs)  122 us
    pallas_call x3, Pallas kernels, attn_bwd(): pl.pallas_call(body, grid=(count,), in_specs=in_specs, out_specs=specs, o...  55.2 us
    pallas_call x1, Pallas kernels, mlp_both(): pl.pallas_call(lambda *refs: mlp_both_body(rows, *refs), grid=(ff // chun...  43.8 us
    pallas_call x3, Pallas kernels, attn_fwd(): pl.pallas_call(lambda *refs: attn_fwd_body(save, at * count, *refs[:used]...  40 us
    ppermute x44, starting transfers between devices, hop(): return lax.ppermute(value, 'dp', pairs)  39 us
    pallas_call x1, Pallas kernels, mlp_grad(): pl.pallas_call(lambda *refs: mlp_grad_body(rows, *refs[:7], *refs[7 + wai...  22.5 us
    pallas_call x1, Pallas kernels, mlp_bwd(): pl.pallas_call(lambda *refs: mlp_bwd_body(save, rows, *refs[:4], *refs[le...  13.5 us
    pallas_call x1, Pallas kernels, mlp_fwd(): pl.pallas_call(lambda *refs: mlp_fwd_body(save, rows, *refs[:6], *refs[6...  13.2 us
  transfers between devices with their start and end apart: 50, of which 25 were waited for; matrix products, arithmetic and copies ran while one was open for 5% of the time, Pallas kernels for 26%

commit v1 on v0

--- a/solution.py
+++ b/solution.py
@@ -170,32 +170,62 @@
         y_ref[...] = acc_ref[...].astype(BF16)
 
 
-def mlp_fwd(c, m, wup, wdown, bup, vec, save, at=0, parts=1, after=(), chunk=1280, rows=256):
+def mlp_fwd(c, m, wup, wdown, bup, vec, at, parts, flag, after=(), chunk=1280, rows=256):
     n, width = c.shape
     n //= parts
+    ff = wup.shape[1]
     waits = len(after)
-    part = pl.BlockSpec((n, width), lambda i: (at, 0))
-    ff = wup.shape[1]
-    outs = [jax.ShapeDtypeStruct((n, width), BF16)]
-    specs = [whole((n, width))]
-    if save:
-        outs += [jax.ShapeDtypeStruct((n, ff), BF16)] * 2
-        specs += [pl.BlockSpec((n, chunk), lambda i: (0, i))] * 2
-    return pl.pallas_call(
-        lambda *refs: mlp_fwd_body(save, rows, *refs[:6], *refs[6 + waits:]),
-        grid=(ff // chunk,),
-        in_specs=[part, part, pl.BlockSpec((width, chunk), lambda i: (0, i)),
-                  pl.BlockSpec((chunk, width), lambda i: (i, 0)), pl.BlockSpec((1, chunk), lambda i: (0, i)), whole(vec.shape)] + tied(waits),
-        out_specs=specs,
-        out_shape=outs,
-        scratch_shapes=[pltpu.VMEM((n, width), F32)],
-        compiler_params=pltpu.CompilerParams(vmem_limit_bytes=VMEM_LIMIT),
-        cost_estimate=cost(26),
+    part = pl.BlockSpec((n, width), lambda i, flag: (at, 0))
+    here = lambda i, flag: i * (1 - flag[0])
+
+    def body(flag_ref, *refs):
+        @pl.when(flag_ref[0] == 0)
+        def _():
+            mlp_fwd_body(False, rows, *refs[:6], *refs[6 + waits:])
+
+    return pl.pallas_call(
+        body,
+        grid_spec=pltpu.PrefetchScalarGridSpec(
+            num_scalar_prefetch=1,
+            grid=(ff // chunk,),
+            in_specs=[part, part, pl.BlockSpec((width, chunk), lambda i, flag: (0, here(i, flag))),
+                      pl.BlockSpec((chunk, width), lambda i, flag: (here(i, flag), 0)),
+                      pl.BlockSpec((1, chunk), lambda i, flag: (0, here(i, flag))), whole(vec.shape)] + tied(waits),
+            out_specs=whole((n, width)),
+            scratch_shapes=[pltpu.VMEM((n, width), F32)],
+        ),
+        out_shape=jax.ShapeDtypeStruct((n, width), BF16),
+        compiler_params=pltpu.CompilerParams(vmem_limit_bytes=VMEM_LIMIT),
+        cost_estimate=cost(13),
         name="feed_forward",
-    )(c, m, wup, wdown, bup, vec, *after)
-
-
-def mlp_both_body(rows, c_ref, m_ref, dz_ref, wup_ref, wdown_ref, bup_ref, vec_ref, y_ref, g_ref, gp_ref, dc_ref, acc_ref):
+    )(flag, c, m, wup, wdown, bup, vec, *after)
+
+
+def pre_grad_body(flag_ref, dz_ref, wdown_ref, dg_ref):
+    @pl.when(flag_ref[0] > 0)
+    def _():
+        dg_ref[...] = dot(dz_ref[...], wdown_ref[...], ((1,), (1,))).astype(BF16)
+
+
+def pre_grad(dz, wdown, flag, after, chunk=1280):
+    n, width = dz.shape
+    ff = wdown.shape[0]
+    return pl.pallas_call(
+        lambda *refs: pre_grad_body(*refs[:3], *refs[3 + len(after):]),
+        grid_spec=pltpu.PrefetchScalarGridSpec(
+            num_scalar_prefetch=1,
+            grid=(ff // chunk,),
+            in_specs=[pl.BlockSpec(dz.shape, lambda i, flag: (0, 0)), pl.BlockSpec((chunk, width), lambda i, flag: (i * flag[0], 0))] + tied(len(after)),
+            out_specs=pl.BlockSpec((n, chunk), lambda i, flag: (0, i * flag[0])),
+        ),
+        out_shape=jax.ShapeDtypeStruct((n, ff), BF16),
+        compiler_params=pltpu.CompilerParams(vmem_limit_bytes=VMEM_LIMIT),
+        cost_estimate=cost(11),
+        name="feed_forward_early_gradient",
+    )(flag, dz, wdown, *after)
+
+
+def mlp_both_body(rows, c_ref, m_ref, dg_ref, wup_ref, wdown_ref, bup_ref, vec_ref, y_ref, g_ref, gp_ref, dc_ref, acc_ref):
     step = pl.program_id(0)
 
     @pl.when(step == 0)
@@ -206,36 +236,35 @@
     for r in range(c_ref.shape[0] // rows):
         at = slice(r * rows, r * rows + rows)
         u = dot(c_ref[at], wup_ref[...]) + bup_ref[...]
-        dg = dot(dz_ref[at], wdown_ref[...], ((1,), (1,)))
         act, slope = gelu_pair(u)
         act, slope = act.astype(BF16), slope.astype(BF16)
         g_ref[at] = act
         gp_ref[at] = slope
         acc_ref[at] += dot(act, wdown_ref[...])
-        dc_ref[at] += dot((dg * slope.astype(F32)).astype(BF16), wup_ref[...], ((1,), (1,)))
+        dc_ref[at] += dot((dg_ref[at].astype(F32) * slope.astype(F32)).astype(BF16), wup_ref[...], ((1,), (1,)))
 
     @pl.when(step == pl.num_programs(0) - 1)
     def _():
         y_ref[...] = acc_ref[...].astype(BF16)
 
 
-def mlp_both(c, m, dz, wup, wdown, bup, vec, chunk=1280, rows=256):
+def mlp_both(c, m, dg, wup, wdown, bup, vec, chunk=1280, rows=256):
     n, width = c.shape
     ff = wup.shape[1]
     column = pl.BlockSpec((n, chunk), lambda i: (0, i))
     return pl.pallas_call(
         lambda *refs: mlp_both_body(rows, *refs),
         grid=(ff // chunk,),
-        in_specs=[whole(c.shape), whole(m.shape), whole(dz.shape), pl.BlockSpec((width, chunk), lambda i: (0, i)),
+        in_specs=[whole(c.shape), whole(m.shape), column, pl.BlockSpec((width, chunk), lambda i: (0, i)),
                   pl.BlockSpec((chunk, width), lambda i: (i, 0)), pl.BlockSpec((1, chunk), lambda i: (0, i)), whole(vec.shape)],
         out_specs=[whole((n, width)), column, column, whole((n, width))],
         out_shape=[jax.ShapeDtypeStruct((n, width), BF16), jax.ShapeDtypeStruct((n, ff), BF16), jax.ShapeDtypeStruct((n, ff), BF16),
                    jax.ShapeDtypeStruct((n, width), F32)],
         scratch_shapes=[pltpu.VMEM((n, width), F32)],
         compiler_params=pltpu.CompilerParams(vmem_limit_bytes=VMEM_LIMIT),
-        cost_estimate=cost(42),
+        cost_estimate=cost(36),
         name="feed_forward_both",
-    )(c, m, dz, wup, wdown, bup, vec)
+    )(c, m, dg, wup, wdown, bup, vec)
 
 
 def mlp_up_body(rows, c_ref, wup_ref, bup_ref, g_ref):
@@ -488,7 +517,7 @@
         [g_gain0, g_gain1, g_shift0, g_shift1, total(dqkv[:, :width]), total(dqkv[:, 2 * width:]), total(dr), total(dz)], axis=0)
 
 
-def attn_bwd(dc, dz, m, h, qkv, e, o, inv, proj, vec, at, parts, grads, earlier=(), after=()):
+def attn_bwd(dc, dz, m, h, qkv, e, o, inv, proj, vec, at, parts, grads, earlier=(), after=(), flag=None):
     n, seq, width = h.shape
     count = n // parts
     row = lambda *tail: pl.BlockSpec((1,) + tail, lambda i: (i + at * count,) + (0,) * len(tail))
@@ -507,12 +536,19 @@
         args += [earlier[3], *earlier[:3]]
         in_specs += [whole(earlier[3].shape)] + tied(3)
     aliases = {base + 1 + i: i for i in range(3)} if earlier else {}
+    if flag is not None:
+        args += [flag]
+        in_specs += [pl.BlockSpec(memory_space=pltpu.SMEM)]
     args += after
     in_specs += tied(len(after))
     used = len(args)
 
     def body(*refs):
-        attn_bwd_body(grads, refs[base] if earlier else None, *refs[:base], *refs[used:])
+        run = lambda: attn_bwd_body(grads, refs[base] if earlier else None, *refs[:base], *refs[used:])
+        if flag is None:
+            run()
+        else:
+            pl.when(refs[base][0] > 0)(run)
 
     return pl.pallas_call(
         body,
@@ -789,19 +825,21 @@
         pieces = [down, down_1, down_2, down_3, down_y0, down_y1, down_y2, down_y3]
         wdown, y_a = place_down(pieces + siblings(pieces, act), to, act, mid, vec)
     else:
-        y_a, = mlp_fwd(c, mid, wup, wdown, bup, vec, False, 0, parts)
-    y_b, = mlp_fwd(c, mid, wup, wdown, bup, vec, False, 1, parts, (y_a,))
+        y_a = mlp_down(act, mid[:n // parts], wdown, vec, 0, 1)
+    flag = section.reshape(1).astype(jnp.int32)
+    early = pre_grad(cotangent.reshape(n, width), wdown, flag, (y_a,))
+    y_b = mlp_fwd(c, mid, wup, wdown, bup, vec, 1, parts, flag, (early,))
     kept = ()
     arrived = [lax.ppermute(y.reshape(part, seq, width), "section", [(0, 1)]) for y in (y_a, y_b)]
     for at in range(parts):
         kept = attn_fwd(tokens, lengths, proj, True, at, parts, held(arrived[at], *kept[:1]), vec, kept)
     m, c, qkv, e, o, a, inv, h = kept
     c = c.reshape(n, width)
-    y, g, gp, dc = mlp_both(c, m.reshape(n, width), cotangent.reshape(n, width), wup, wdown, bup, vec)
+    y, g, gp, dc = mlp_both(c, m.reshape(n, width), early, wup, wdown, bup, vec)
     dc = dc.reshape(tokens.shape)
     arrived = []
     for at in range(parts):
-        back, = attn_bwd(dc, cotangent, m, h, qkv, e, o, inv, proj, vec, at, parts, False)
+        back, = attn_bwd(dc, cotangent, m, h, qkv, e, o, inv, proj, vec, at, parts, False, flag=flag)
         arrived.append(lax.ppermute(back, "section", [(1, 0)]))
     dz = [jnp.where(section == 1, cotangent[:part], arrived[0])]
     dc, du = mlp_bwd(dz[0].reshape(part * seq, width), gp, wup, wdown, True, 0, parts)

time: 466 us -> 463 us (level)
  Pallas kernels: 240 us -> 220 us
  waiting for transfers between devices: 127 us -> 144 us
    ppermute x2, waiting for transfers between devices: 2.35 us -> 19.2 us  [on_device(): arrived.append(lax.ppermute(back, 'section', [(1, 0)]))]
    pallas_call x3, Pallas kernels: 55.2 us -> 38.6 us  [attn_bwd(): pl.pallas_call(body, grid=(count,), in_specs=in_specs, out_specs=specs, o...]
    pallas_call x1, Pallas kernels: 43.8 us -> 37.3 us  [mlp_both(): pl.pallas_call(lambda *refs: mlp_both_body(rows, *refs), grid=(ff // chun...]
    pallas_call x1 -> x2, Pallas kernels: 13.2 us -> 16.7 us  [the longest x1 13.2 us: mlp_fwd(): pl.pallas_call(body, grid_spec=pltpu.PrefetchScalarGridSpec(num_scalar_pr...]
where the time goes in v1:
time: 463 us; the launch traced here: 454 us
  Pallas kernels  220 us (48%)
  waiting for transfers between devices  144 us (31%)
  starting transfers between devices  47.4 us (10%)
  other arithmetic  17.5 us (4%)
  between operations  14.8 us (3%)
  local copies, waits for them, and re-layouts  10.4 us (2%)
    ppermute x44, waiting for transfers between devices, hop(): return lax.ppermute(value, 'dp', pairs)  122 us
    pallas_call x3, Pallas kernels, attn_fwd(): pl.pallas_call(lambda *refs: attn_fwd_body(save, at * count, *refs[:used]...  39.9 us
    ppermute x44, starting transfers between devices, hop(): return lax.ppermute(value, 'dp', pairs)  39.4 us
    pallas_call x3, Pallas kernels, attn_bwd(): pl.pallas_call(body, grid=(count,), in_specs=in_specs, out_specs=specs, o...  38.6 us
    pallas_call x1, Pallas kernels, mlp_both(): pl.pallas_call(lambda *refs: mlp_both_body(rows, *refs), grid=(ff // chun...  37.3 us
    pallas_call x1, Pallas kernels, mlp_grad(): pl.pallas_call(lambda *refs: mlp_grad_body(rows, *refs[:7], *refs[7 + wai...  22.4 us
    ppermute x2, waiting for transfers between devices, on_device(): arrived.append(lax.ppermute(back, 'section', [(1, 0)]))  19.2 us
    pallas_call x1, Pallas kernels, mlp_bwd(): pl.pallas_call(lambda *refs: mlp_bwd_body(save, rows, *refs[:4], *refs[le...  13.4 us
  transfers between devices with their start and end apart: 50, of which 25 were waited for; matrix products, arithmetic and copies ran while one was open for 5% of the time, Pallas kernels for 26%

profile of v1, /device:TPU:0, one launch (start us, length us, event | category | flops | bytes accessed | tf_op | source)
XLA Modules:
  0.0 454.1 jit_solution(2857557994735515470)
XLA Ops:
  10.6 3.0 collective-permute-start.2
  13.7 3.6 collective-permute-start.1
  19.0 5.1 %collective-permute-done.1.refs_4_ = bf16[40,2688]{1,0:T(8,128)(2,1)S(1)} collective-permute-done((bf16[40,2688]{1,0:T(8,128)(2,1)S(1)}, bf16[40,2688]{1,0:T(8,128)(2,1)S(1)}, u32[]{:S(2)}, u32[]{:S(2)}) %collective-permute-start.1) | collective-permute-done | bytes 215072 | tf_op jit(solution)/shard_map/ppermute | solution.py:712
  24.1 8.2 %collective-permute-done.refs_2_ = bf16[40,2688]{1,0:T(8,128)(2,1)S(1)} collective-permute-done((bf16[40,2688]{1,0:T(8,128)(2,1)S(1)}, bf16[40,2688]{1,0:T(8,128)(2,1)S(1)}, u32[]{:S(2)}, u32[]{:S(2)}) %collective-permute-start) | collective-permute-done | bytes 215072 | tf_op jit(solution)/shard_map/ppermute | solution.py:712
  34.8 3.5 collective-permute-start.3
  40.3 18.0 %collective-permute-done.3.refs_3_ = bf16[40,2688]{1,0:T(8,128)(2,1)S(1)} collective-permute-done((bf16[40,2688]{1,0:T(8,128)(2,1)S(1)}, bf16[40,2688]{1,0:T(8,128)(2,1)S(1)}, u32[]{:S(2)}, u32[]{:S(2)}) %collective-permute-start.3) | collective-permute-done | bytes 215072 | tf_op jit(solution)/shard_map/ppermute | solution.py:712
  62.0 8.8 %collective-permute-done.8.refs_7_ = bf16[40,2688]{1,0:T(8,128)(2,1)} collective-permute-done((bf16[40,2688]{1,0:T(8,128)(2,1)S(1)}, bf16[40,2688]{1,0:T(8,128)(2,1)}, u32[]{:S(2)}, u32[]{:S(2)}) %collective-permute-start.8) | collective-permute-done | bytes 215072 | tf_op jit(solution)/shard_map/ppermute | solution.py:712
  71.2 13.9 %collective-permute-done.17.refs_7_ = bf16[320,640]{1,0:T(8,128)(2,1)S(1)} collective-permute-done((bf16[320,640]{1,0:T(8,128)(2,1)}, bf16[320,640]{1,0:T(8,128)(2,1)S(1)}, u32[]{:S(2)}, u32[]{:S(2)}) %collective-permute-start.17) | collective-permute-done | bytes 409632 | tf_op jit(solution)/shard_map/ppermute | solution.py:712
  91.2 5.0 %place_pieces.1 = bf16[16,40,2688]{2,1,0:T(8,128)(2,1)} custom-call(s32[16]{0:T(128)} %stack.67.refs_0_, bf16[40,2688]{1,0:T(8,128)(2,1)} %copy-done.8, bf16[40,2688]{1,0:T(8,128)(2,1)} %copy-done.27, bf16[40,2688]{1,0:T(8,128)(2,1)} %copy-done.28, bf16[40,2688]{1,0:T(8,128)(2,1)} %copy-done.26, bf16[40,2688]{1,0:T(8,128)(2,1)} %copy-done.25, ...), custom_call_target="tpu_custom_call" | custom-call | flops 4400000000 | bytes 1024 | tf_op jit(solution)/shard_map/place_pieces/pallas_call | solution.py:616
  98.8 16.7 %attention_forward.3 = (f32[4,256,640]{2,1,0:T(8,128)}, bf16[4,256,640]{2,1,0:T(8,128)(2,1)}) custom-call(s32[5]{0:T(128)} %pad_add_fusion.refs_0_, bf16[4,256,640]{2,1,0:T(8,128)(2,1)} %refs_1_.7, bf16[640,2688]{1,0:T(8,128)(2,1)} %bitcast.57, f32[8,640]{1,0:T(8,128)} %convert_bitcast_fusion.refs_3_.refs_5_.refs_4_.refs_6_.refs_9_, ...), custom_call_target="tpu_custom_call" | custom-call | flops 19800000512 | bytes 1024 | tf_op jit(solution)/shard_map/attention_forward/pallas_call | solution.py:131
  119.3 8.6 %feed_forward_up.1.refs_1_ = bf16[512,5120]{1,0:T(8,128)(2,1)} custom-call(bf16[1024,640]{1,0:T(8,128)(2,1)} %bitcast.89, bf16[640,5120]{1,0:T(8,128)(2,1)} %bitcast.67, f32[1,5120]{1,0:T(1,128)} %reshape.201.refs_4_.refs_2_.refs_5_), custom_call_target="tpu_custom_call" | custom-call | flops 7040000000 | bytes 1024 | tf_op jit(solution)/shard_map/feed_forward_up/pallas_call | solution.py:281
  134.5 11.0 %place_and_feed_forward_down.1 = (bf16[5120,640]{1,0:T(8,128)(2,1)}, bf16[512,640]{1,0:T(8,128)(2,1)}) custom-call(s32[16]{0:T(128)} %stack.67.refs_0_, bf16[512,5120]{1,0:T(8,128)(2,1)} %feed_forward_up.1.refs_1_, f32[1024,640]{1,0:T(8,128)} %bitcast.82, f32[8,640]{1,0:T(8,128)} %convert_bitcast_fusion.refs_3_.refs_5_.refs_4_.refs_6_.refs_9_, ...), custom_call_target="tpu_custom_call" | custom-call | flops 11000000512 | bytes 1024 | tf_op jit(solution)/shard_map/place_and_feed_forward_down/pallas_call | solution.py:650
  145.6 3.9 collective-permute-start.31
  149.5 3.5 feed_forward_early_gradient.1.refs_6_.refs_2_
  152.9 13.2 %feed_forward.1 = bf16[512,640]{1,0:T(8,128)(2,1)} custom-call(s32[1]{0:T(128)} %bitcast.refs_0_.flag_ref.refs_10_, bf16[1024,640]{1,0:T(8,128)(2,1)} %bitcast.90, f32[1024,640]{1,0:T(8,128)} %bitcast.83, bf16[640,5120]{1,0:T(8,128)(2,1)} %bitcast.68, bf16[5120,640]{1,0:T(8,128)(2,1)} %get-tuple-element.114.refs_2_.refs_3_.refs_4_, ...), custom_call_target="tpu_custom_call" | custom-call | flops 14300000256 | bytes 1024 | tf_op jit(solution)/shard_map/feed_forward/pallas_call | solution.py:186
  168.3 11.6 %attention_forward.4 = (f32[4,256,640]{2,1,0:T(8,128)}, bf16[4,256,640]{2,1,0:T(8,128)(2,1)}, bf16[4,256,1920]{2,1,0:T(8,128)(2,1)}, bf16[4,20,256,256]{3,2,1,0:...) custom-call(s32[5]{0:T(128)} %pad_add_fusion.refs_0_, ...), custom_call_target="tpu_custom_call" | custom-call | flops 9900000256 | bytes 1024 | tf_op jit(solution)/shard_map/attention_forward/pallas_call | solution.py:131
  183.0 11.6 %attention_forward.5 = (f32[4,256,640]{2,1,0:T(8,128)}, bf16[4,256,640]{2,1,0:T(8,128)(2,1)}, bf16[4,256,1920]{2,1,0:T(8,128)(2,1)}, bf16[4,20,256,256]{3,2,1,0:...) custom-call(s32[5]{0:T(128)} %pad_add_fusion.refs_0_, ...), custom_call_target="tpu_custom_call", output_to_operand_aliasing={{0}: (5, {}), {1}: (6, {}), {2}: (7, {}), {3}: (8, {}), {4}... | custom-call | flops 9900000256 | bytes 1024 | tf_op jit(solution)/shard_map/attention_forward/pallas_call | solution.py:131
  194.7 37.3 %feed_forward_both.1 = (bf16[1024,640]{1,0:T(8,128)(2,1)}, bf16[1024,5120]{1,0:T(8,128)(2,1)}, bf16[1024,5120]{1,0:T(8,128)(2,1)}, f32[1024,640]{1,0:T(8,128)}) custom-call(bf16[1024,640]{1,0:T(8,128)(2,1)} %bitcast.92, f32[1024,640]{1,0:T(8,128)} %bitcast.84, bf16[1024,5120]{1,0:T(8,128)(2,1)} %feed_forward_early_gradient.1.refs_6_.refs_2_, ...), custom_call_target="tpu_custom_call" | custom-call | flops 39600001024 | bytes 1024 | tf_op jit(solution)/shard_map/feed_forward_both/pallas_call | solution.py:255
  232.0 6.5 %attention_back.4 = bf16[2,256,640]{2,1,0:T(8,128)(2,1)} custom-call(f32[4,256,640]{2,1,0:T(8,128)} %bitcast.86, bf16[4,256,640]{2,1,0:T(8,128)(2,1)} %refs_1_.9, f32[4,256,640]{2,1,0:T(8,128)} %get-tuple-element.126.refs_2_, bf16[4,256,640]{2,1,0:T(8,128)(2,1)} %get-tuple-element.129.refs_3_, bf16[4,256,1920]{2,1,0:T(8,128)(2,1)} %get-tuple-element.130.refs_4_, ...), custom_call_target="tpu_custom_call" | custom-call | flops 15399999488 | bytes 1024 | tf_op jit(solution)/shard_map/attention_back/pallas_call | solution.py:553
  239.9 6.7 %attention_back.3 = bf16[2,256,640]{2,1,0:T(8,128)(2,1)} custom-call(f32[4,256,640]{2,1,0:T(8,128)} %bitcast.87, bf16[4,256,640]{2,1,0:T(8,128)(2,1)} %refs_1_.9, f32[4,256,640]{2,1,0:T(8,128)} %get-tuple-element.126.refs_2_, bf16[4,256,640]{2,1,0:T(8,128)(2,1)} %get-tuple-element.129.refs_3_, bf16[4,256,1920]{2,1,0:T(8,128)(2,1)} %get-tuple-element.130.refs_4_, ...), custom_call_target="tpu_custom_call" | custom-call | flops 15399999488 | bytes 1024 | tf_op jit(solution)/shard_map/attention_back/pallas_call | solution.py:553
  247.8 17.3 %collective-permute-done.33 = bf16[2,256,640]{2,1,0:T(8,128)(2,1)S(1)} collective-permute-done((bf16[2,256,640]{2,1,0:T(8,128)(2,1)}, bf16[2,256,640]{2,1,0:T(8,128)(2,1)S(1)}, u32[]{:S(2)}, u32[]{:S(2)}) %collective-permute-start.33) | collective-permute-done | bytes 655392 | tf_op jit(solution)/shard_map/ppermute | solution.py:843
  266.0 13.4 %feed_forward_back.1 = (f32[1024,640]{1,0:T(8,128)}, bf16[512,5120]{1,0:T(8,128)(2,1)}) custom-call(bf16[512,640]{1,0:T(8,128)(2,1)} %bitcast.50, bf16[1024,5120]{1,0:T(8,128)(2,1)} %get-tuple-element.134.refs_1_, bf16[640,5120]{1,0:T(8,128)(2,1)} %bitcast.70, bf16[5120,640]{1,0:T(8,128)(2,1)} %get-tuple-element.114.refs_2_.refs_3_.refs_4_), custom_call_target="tpu_custom_call" | custom-call | flops 12099999744 | bytes 1024 | tf_op jit(solution)/shard_map/feed_forward_back/pallas_call | solution.py:348
  282.7 12.4 %down_gradient.1.refs_8_ = bf16[5120,640]{1,0:T(8,128)(2,1)} custom-call(bf16[1024,5120]{1,0:T(8,128)(2,1)} %get-tuple-element.138.refs_0_, bf16[1024,640]{1,0:T(8,128)(2,1)} %bitcast.52), custom_call_target="tpu_custom_call" | custom-call | flops 13200000000 | bytes 1024 | tf_op jit(solution)/shard_map/down_gradient/pallas_call | solution.py:446
  295.1 22.4 %feed_forward_gradients.1 = (f32[1024,640]{1,0:T(8,128)}, bf16[320,5120]{1,0:T(8,128)(2,1)}, bf16[320,5120]{1,0:T(8,128)(2,1)}, f32[8,5120]{1,0:T(8,128)}) custom-call(bf16[512,640]{1,0:T(8,128)(2,1)} %bitcast.49, bf16[1024,5120]{1,0:T(8,128)(2,1)} %get-tuple-element.134.refs_1_, bf16[640,5120]{1,0:T(8,128)(2,1)} %bitcast.71, ...), custom_call_target="tpu_custom_call", output_to_operand_aliasing={{0}: (7, {})} | custom-call | flops 23100000256 | bytes 1024 | tf_op jit(solution)/shard_map/feed_forward_gradients/pallas_call | solution.py:423
  328.7 25.5 %attention_back.5 = (f32[4,256,640]{2,1,0:T(8,128)}, bf16[4,256,640]{2,1,0:T(8,128)(2,1)}, bf16[4,256,1920]{2,1,0:T(8,128)(2,1)}, f32[8,640]{1,0:T(8,128)}) custom-call(f32[4,256,640]{2,1,0:T(8,128)} %bitcast.85, bf16[4,256,640]{2,1,0:T(8,128)(2,1)} %pad_maximum_fusion.refs_1_, f32[4,256,640]{2,1,0:T(8,128)} %get-tuple-element.126.refs_2_, ...), custom_call_target="tpu_custom_call" | custom-call | flops 30799998976 | bytes 1024 | tf_op jit(solution)/shard_map/attention_back/pallas_call | solution.py:553
  358.0 11.7 %projection_gradients.1 = (bf16[320,2688]{1,0:T(8,128)(2,1)}, bf16[320,2688]{1,0:T(8,128)(2,1)}) custom-call(bf16[1024,640]{1,0:T(8,128)(2,1)} %bitcast.95, bf16[1024,1920]{1,0:T(8,128)(2,1)} %bitcast.80, bf16[1024,640]{1,0:T(8,128)(2,1)} %bitcast.94, bf16[1024,640]{1,0:T(8,128)(2,1)} %bitcast.91, f32[8,640]{1,0:T(8,128)} %get-tuple-element.145.refs_4_, ...), custom_call_target="tpu_custom_call" | custom-call | flops 9900000256 | bytes 1024 | tf_op jit(solution)/shard_map/projection_gradients/pallas_call | solution.py:590
  369.7 9.5 %collective-permute-done.36 = bf16[160,2560]{1,0:T(8,128)(2,1)S(1)} collective-permute-done((bf16[160,2560]{1,0:T(8,128)(2,1)S(1)}, bf16[160,2560]{1,0:T(8,128)(2,1)S(1)}, u32[]{:S(2)}, u32[]{:S(2)}) %collective-permute-start.36) | collective-permute-done | bytes 819232 | tf_op jit(solution)/shard_map/ppermute | solution.py:712
  383.4 5.4 %collective-permute-start.43 = (bf16[40,2560]{1,0:T(8,128)(2,1)S(1)}, bf16[40,2560]{1,0:T(8,128)(2,1)S(1)}, u32[]{:S(2)}, u32[]{:S(2)}) collective-permute-start(bf16[40,2560]{1,0:T(8,128)(2,1)S(1)} %get-tuple-element.163), channel_id=1, source_target_pairs={{0,8},{1,9},{2,10},{3,11},{4,12},{5,13},{6,14},{7,15},{8,0},{9,1},... | collective-permute-start | bytes 614408 | tf_op jit(solution)/shard_map/ppermute | solution.py:712
  391.5 5.3 %collective-permute-done.44 = bf16[40,2560]{1,0:T(8,128)(2,1)S(1)} collective-permute-done((bf16[40,2560]{1,0:T(8,128)(2,1)S(1)}, bf16[40,2560]{1,0:T(8,128)(2,1)S(1)}, u32[]{:S(2)}, u32[]{:S(2)}) %collective-permute-start.44) | collective-permute-done | bytes 204832 | tf_op jit(solution)/shard_map/ppermute | solution.py:712
  396.8 13.6 %collective-permute-done.43 = bf16[40,2560]{1,0:T(8,128)(2,1)S(1)} collective-permute-done((bf16[40,2560]{1,0:T(8,128)(2,1)S(1)}, bf16[40,2560]{1,0:T(8,128)(2,1)S(1)}, u32[]{:S(2)}, u32[]{:S(2)}) %collective-permute-start.43) | collective-permute-done | bytes 204832 | tf_op jit(solution)/shard_map/ppermute | solution.py:712
  418.1 8.6 %collective-permute-done.47.refs_5_ = bf16[40,2688]{1,0:T(8,128)(2,1)S(1)} collective-permute-done((bf16[40,2688]{1,0:T(8,128)(2,1)S(1)}, bf16[40,2688]{1,0:T(8,128)(2,1)S(1)}, u32[]{:S(2)}, u32[]{:S(2)}) %collective-permute-start.47) | collective-permute-done | bytes 215072 | tf_op jit(solution)/shard_map/ppermute | solution.py:712
  426.7 16.4 %collective-permute-done.46.refs_4_ = bf16[40,2688]{1,0:T(8,128)(2,1)S(1)} collective-permute-done((bf16[40,2688]{1,0:T(8,128)(2,1)S(1)}, bf16[40,2688]{1,0:T(8,128)(2,1)S(1)}, u32[]{:S(2)}, u32[]{:S(2)}) %collective-permute-start.46) | collective-permute-done | bytes 215072 | tf_op jit(solution)/shard_map/ppermute | solution.py:712
  (185 shorter events, 78.1 us)
Async XLA Ops:
  7.2 112.1 %all-gather.3.cloned.1.call-start = ((), (), s32[]{:S(2)}) async-start(), calls=%async_computation.2 | async-start | bytes 6963200 | tf_op jit(solution)/shard_map/all_gather | solution.py:793
  7.9 435.2 %reduce-scatter.2.cloned.1.call-start = ((), (), s32[]{:S(2)}) async-start(), calls=%async_computation.1 | async-start | bytes 6963200 | tf_op jit(solution)/shard_map/reduce_scatter | solution.py:850
  17.3 15.0 %collective-permute-start = (bf16[40,2688]{1,0:T(8,128)(2,1)S(1)}, bf16[40,2688]{1,0:T(8,128)(2,1)S(1)}, u32[]{:S(2)}, u32[]{:S(2)}) collective-permute-start(bf16[40,2688]{1,0:T(8,128)(2,1)S(1)} %pad_maximum_fusion.1.refs_1_), channel_id=1, source_target_pairs={{0,4},{1,5},{2,6},{3,7},{4,8},{5,9},{6,10},{7,11},{8,12},{9,13},{1... | collective-permute-start | bytes 645128 | tf_op jit(solution)/shard_map/ppermute | solution.py:712
  17.3 23.0 %collective-permute-start.6 = (bf16[320,640]{1,0:T(8,128)(2,1)}, bf16[320,640]{1,0:T(8,128)(2,1)S(1)}, u32[]{:S(2)}, u32[]{:S(2)}) collective-permute-start(bf16[320,640]{1,0:T(8,128)(2,1)} %bitcast.74), channel_id=1, source_target_pairs={{0,2},{1,3},{2,0},{3,1},{4,6},{5,7},{6,4},{7,5},{8,10},{9,11},{10,... | collective-permute-start | bytes 1228808 | tf_op jit(solution)/shard_map/ppermute | solution.py:712
  32.3 26.0 %collective-permute-start.7 = (bf16[320,640]{1,0:T(8,128)(2,1)}, bf16[320,640]{1,0:T(8,128)(2,1)S(1)}, u32[]{:S(2)}, u32[]{:S(2)}) collective-permute-start(bf16[320,640]{1,0:T(8,128)(2,1)} %bitcast.75), channel_id=1, source_target_pairs={{0,4},{1,5},{2,6},{3,7},{4,8},{5,9},{6,10},{7,11},{8,12},{9,13},{1... | collective-permute-start | bytes 1228808 | tf_op jit(solution)/shard_map/ppermute | solution.py:712
  34.8 23.5 %collective-permute-start.3 = (bf16[40,2688]{1,0:T(8,128)(2,1)S(1)}, bf16[40,2688]{1,0:T(8,128)(2,1)S(1)}, u32[]{:S(2)}, u32[]{:S(2)}) collective-permute-start(bf16[40,2688]{1,0:T(8,128)(2,1)S(1)} %pad_maximum_fusion.1.refs_1_), channel_id=1, source_target_pairs={{0,8},{1,9},{2,10},{3,11},{4,12},{5,13},{6,14},{7,15},{8,0},{9,1},... | collective-permute-start | bytes 645128 | tf_op jit(solution)/shard_map/ppermute | solution.py:712
  38.2 20.0 %collective-permute-start.4 = (bf16[40,2688]{1,0:T(8,128)(2,1)S(1)}, bf16[40,2688]{1,0:T(8,128)(2,1)}, u32[]{:S(2)}, u32[]{:S(2)}) collective-permute-start(bf16[40,2688]{1,0:T(8,128)(2,1)S(1)} %collective-permute-done.refs_2_), channel_id=1, source_target_pairs={{0,2},{1,3},{2,0},{3,1},{4,6},{5,7},{6,4},{7,5},{8,10},{9,11},{10,... | collective-permute-start | bytes 645128 | tf_op jit(solution)/shard_map/ppermute | solution.py:712
  38.2 20.0 %collective-permute-start.5 = (bf16[40,2688]{1,0:T(8,128)(2,1)S(1)}, bf16[40,2688]{1,0:T(8,128)(2,1)}, u32[]{:S(2)}, u32[]{:S(2)}) collective-permute-start(bf16[40,2688]{1,0:T(8,128)(2,1)S(1)} %collective-permute-done.1.refs_4_), channel_id=1, source_target_pairs={{0,2},{1,3},{2,0},{3,1},{4,6},{5,7},{6,4},{7,5},{8,10},{9,11},{10,... | collective-permute-start | bytes 645128 | tf_op jit(solution)/shard_map/ppermute | solution.py:712
  58.3 12.4 %collective-permute-start.8 = (bf16[40,2688]{1,0:T(8,128)(2,1)S(1)}, bf16[40,2688]{1,0:T(8,128)(2,1)}, u32[]{:S(2)}, u32[]{:S(2)}) collective-permute-start(bf16[40,2688]{1,0:T(8,128)(2,1)S(1)} %collective-permute-done.3.refs_3_), channel_id=1, source_target_pairs={{0,2},{1,3},{2,0},{3,1},{4,6},{5,7},{6,4},{7,5},{8,10},{9,11},{10,... | collective-permute-start | bytes 645128 | tf_op jit(solution)/shard_map/ppermute | solution.py:712
  58.9 26.2 %collective-permute-start.17 = (bf16[320,640]{1,0:T(8,128)(2,1)}, bf16[320,640]{1,0:T(8,128)(2,1)S(1)}, u32[]{:S(2)}, u32[]{:S(2)}) collective-permute-start(bf16[320,640]{1,0:T(8,128)(2,1)} %bitcast.76), channel_id=1, source_target_pairs={{0,12},{1,13},{2,14},{3,15},{4,0},{5,1},{6,2},{7,3},{8,4},{9,5},{1... | collective-permute-start | bytes 1228808 | tf_op jit(solution)/shard_map/ppermute | solution.py:712
  60.4 26.1 %collective-permute-start.18 = (bf16[320,640]{1,0:T(8,128)(2,1)S(1)}, bf16[320,640]{1,0:T(8,128)(2,1)S(1)}, u32[]{:S(2)}, u32[]{:S(2)}) collective-permute-start(bf16[320,640]{1,0:T(8,128)(2,1)S(1)} %collective-permute-done.7.refs_5_), channel_id=1, source_target_pairs={{0,2},{1,3},{2,0},{3,1},{4,6},{5,7},{6,4},{7,5},{8,10},{9,11},{10,... | collective-permute-start | bytes 1228808 | tf_op jit(solution)/shard_map/ppermute | solution.py:712
  70.7 15.8 %collective-permute-start.9 = (bf16[40,2688]{1,0:T(8,128)(2,1)S(1)}, bf16[40,2688]{1,0:T(8,128)(2,1)S(1)}, u32[]{:S(2)}, u32[]{:S(2)}) collective-permute-start(bf16[40,2688]{1,0:T(8,128)(2,1)S(1)} %pad_maximum_fusion.1.refs_1_), channel_id=1, source_target_pairs={{0,1},{1,0},{2,3},{3,2},{4,5},{5,4},{6,7},{7,6},{8,9},{9,8},{10,11... | collective-permute-start | bytes 645128 | tf_op jit(solution)/shard_map/ppermute | solution.py:712
  70.7 16.3 %collective-permute-start.10 = (bf16[40,2688]{1,0:T(8,128)(2,1)S(1)}, bf16[40,2688]{1,0:T(8,128)(2,1)S(1)}, u32[]{:S(2)}, u32[]{:S(2)}) collective-permute-start(bf16[40,2688]{1,0:T(8,128)(2,1)S(1)} %collective-permute-done.refs_2_), channel_id=1, source_target_pairs={{0,1},{1,0},{2,3},{3,2},{4,5},{5,4},{6,7},{7,6},{8,9},{9,8},{10,11... | collective-permute-start | bytes 645128 | tf_op jit(solution)/shard_map/ppermute | solution.py:712
  71.2 15.9 %collective-permute-start.11 = (bf16[40,2688]{1,0:T(8,128)(2,1)S(1)}, bf16[40,2688]{1,0:T(8,128)(2,1)S(1)}, u32[]{:S(2)}, u32[]{:S(2)}) collective-permute-start(bf16[40,2688]{1,0:T(8,128)(2,1)S(1)} %collective-permute-done.3.refs_3_), channel_id=1, source_target_pairs={{0,1},{1,0},{2,3},{3,2},{4,5},{5,4},{6,7},{7,6},{8,9},{9,8},{10,11... | collective-permute-start | bytes 645128 | tf_op jit(solution)/shard_map/ppermute | solution.py:712
  90.1 27.5 %collective-permute-start.19 = (bf16[320,640]{1,0:T(8,128)(2,1)}, bf16[320,640]{1,0:T(8,128)(2,1)S(1)}, u32[]{:S(2)}, u32[]{:S(2)}) collective-permute-start(bf16[320,640]{1,0:T(8,128)(2,1)} %bitcast.77), channel_id=1, source_target_pairs={{0,8},{1,9},{2,10},{3,11},{4,12},{5,13},{6,14},{7,15},{8,0},{9,1},... | collective-permute-start | bytes 1228808 | tf_op jit(solution)/shard_map/ppermute | solution.py:712
  90.2 27.4 %collective-permute-start.20 = (bf16[320,640]{1,0:T(8,128)(2,1)S(1)}, bf16[320,640]{1,0:T(8,128)(2,1)S(1)}, u32[]{:S(2)}, u32[]{:S(2)}) collective-permute-start(bf16[320,640]{1,0:T(8,128)(2,1)S(1)} %collective-permute-done.17.refs_7_), channel_id=1, source_target_pairs={{0,2},{1,3},{2,0},{3,1},{4,6},{5,7},{6,4},{7,5},{8,10},{9,11},{10,... | collective-permute-start | bytes 1228808 | tf_op jit(solution)/shard_map/ppermute | solution.py:712
  145.6 21.9 %collective-permute-start.31 = (bf16[2,256,640]{2,1,0:T(8,128)(2,1)}, bf16[2,256,640]{2,1,0:T(8,128)(2,1)S(1)}, u32[]{:S(2)}, u32[]{:S(2)}) collective-permute-start(bf16[2,256,640]{2,1,0:T(8,128)(2,1)} %bitcast.72), channel_id=1, source_target_pairs={{0,16},{1,17},{2,18},{3,19},{4,20},{5,21},{6,22},{7,23},{8,24},{9,... | collective-permute-start | bytes 1966088 | tf_op jit(solution)/shard_map/ppermute | solution.py:833
  166.2 16.0 %collective-permute-start.30 = (bf16[2,256,640]{2,1,0:T(8,128)(2,1)}, bf16[2,256,640]{2,1,0:T(8,128)(2,1)S(1)}, u32[]{:S(2)}, u32[]{:S(2)}) collective-permute-start(bf16[2,256,640]{2,1,0:T(8,128)(2,1)} %bitcast.73), channel_id=1, source_target_pairs={{0,16},{1,17},{2,18},{3,19},{4,20},{5,21},{6,22},{7,23},{8,24},{9,... | collective-permute-start | bytes 1966088 | tf_op jit(solution)/shard_map/ppermute | solution.py:833
  238.4 26.6 %collective-permute-start.33 = (bf16[2,256,640]{2,1,0:T(8,128)(2,1)}, bf16[2,256,640]{2,1,0:T(8,128)(2,1)S(1)}, u32[]{:S(2)}, u32[]{:S(2)}) collective-permute-start(bf16[2,256,640]{2,1,0:T(8,128)(2,1)} %attention_back.4), channel_id=1, source_target_pairs={{16,0},{17,1},{18,2},{19,3},{20,4},{21,5},{22,6},{23,7},{24,8},{25... | collective-permute-start | bytes 1966088 | tf_op jit(solution)/shard_map/ppermute | solution.py:843
  246.5 34.8 %collective-permute-start.32 = (bf16[2,256,640]{2,1,0:T(8,128)(2,1)}, bf16[2,256,640]{2,1,0:T(8,128)(2,1)S(1)}, u32[]{:S(2)}, u32[]{:S(2)}) collective-permute-start(bf16[2,256,640]{2,1,0:T(8,128)(2,1)} %attention_back.3), channel_id=1, source_target_pairs={{16,0},{17,1},{18,2},{19,3},{20,4},{21,5},{22,6},{23,7},{24,8},{25... | collective-permute-start | bytes 1966088 | tf_op jit(solution)/shard_map/ppermute | solution.py:843
  325.2 29.0 %collective-permute-start.35 = (bf16[160,2560]{1,0:T(8,128)(2,1)S(1)}, bf16[160,2560]{1,0:T(8,128)(2,1)S(1)}, u32[]{:S(2)}, u32[]{:S(2)}) collective-permute-start(bf16[160,2560]{1,0:T(8,128)(2,1)S(1)} %add_convert_fusion.2), channel_id=1, source_target_pairs={{0,2},{1,3},{2,0},{3,1},{4,6},{5,7},{6,4},{7,5},{8,10},{9,11},{10,... | collective-permute-start | bytes 2457608 | tf_op jit(solution)/shard_map/ppermute | solution.py:712
  327.4 51.9 %collective-permute-start.36 = (bf16[160,2560]{1,0:T(8,128)(2,1)S(1)}, bf16[160,2560]{1,0:T(8,128)(2,1)S(1)}, u32[]{:S(2)}, u32[]{:S(2)}) collective-permute-start(bf16[160,2560]{1,0:T(8,128)(2,1)S(1)} %add_convert_fusion.1), channel_id=1, source_target_pairs={{0,2},{1,3},{2,0},{3,1},{4,6},{5,7},{6,4},{7,5},{8,10},{9,11},{10,... | collective-permute-start | bytes 2457608 | tf_op jit(solution)/shard_map/ppermute | solution.py:712
  355.9 23.4 %collective-permute-start.39 = (bf16[40,2560]{1,0:T(8,128)(2,1)S(1)}, bf16[40,2560]{1,0:T(8,128)(2,1)S(1)}, u32[]{:S(2)}, u32[]{:S(2)}) collective-permute-start(bf16[40,2560]{1,0:T(8,128)(2,1)S(1)} %get-tuple-element.165), channel_id=1, source_target_pairs={{0,12},{1,13},{2,14},{3,15},{4,0},{5,1},{6,2},{7,3},{8,4},{9,5},{1... | collective-permute-start | bytes 614408 | tf_op jit(solution)/shard_map/ppermute | solution.py:712
  357.1 24.4 %collective-permute-start.38 = (bf16[40,2560]{1,0:T(8,128)(2,1)S(1)}, bf16[40,2560]{1,0:T(8,128)(2,1)S(1)}, u32[]{:S(2)}, u32[]{:S(2)}) collective-permute-start(bf16[40,2560]{1,0:T(8,128)(2,1)S(1)} %get-tuple-element.166), channel_id=1, source_target_pairs={{0,8},{1,9},{2,10},{3,11},{4,12},{5,13},{6,14},{7,15},{8,0},{9,1},... | collective-permute-start | bytes 614408 | tf_op jit(solution)/shard_map/ppermute | solution.py:712
  357.1 24.4 %collective-permute-start.37 = (bf16[40,2560]{1,0:T(8,128)(2,1)S(1)}, bf16[40,2560]{1,0:T(8,128)(2,1)S(1)}, u32[]{:S(2)}, u32[]{:S(2)}) collective-permute-start(bf16[40,2560]{1,0:T(8,128)(2,1)S(1)} %get-tuple-element.167), channel_id=1, source_target_pairs={{0,4},{1,5},{2,6},{3,7},{4,8},{5,9},{6,10},{7,11},{8,12},{9,13},{1... | collective-permute-start | bytes 614408 | tf_op jit(solution)/shard_map/ppermute | solution.py:712
  383.3 13.5 %collective-permute-start.44 = (bf16[40,2560]{1,0:T(8,128)(2,1)S(1)}, bf16[40,2560]{1,0:T(8,128)(2,1)S(1)}, u32[]{:S(2)}, u32[]{:S(2)}) collective-permute-start(bf16[40,2560]{1,0:T(8,128)(2,1)S(1)} %get-tuple-element.162), channel_id=1, source_target_pairs={{0,12},{1,13},{2,14},{3,15},{4,0},{5,1},{6,2},{7,3},{8,4},{9,5},{1... | collective-permute-start | bytes 614408 | tf_op jit(solution)/shard_map/ppermute | solution.py:712
  383.4 27.0 %collective-permute-start.43 = (bf16[40,2560]{1,0:T(8,128)(2,1)S(1)}, bf16[40,2560]{1,0:T(8,128)(2,1)S(1)}, u32[]{:S(2)}, u32[]{:S(2)}) collective-permute-start(bf16[40,2560]{1,0:T(8,128)(2,1)S(1)} %get-tuple-element.163), channel_id=1, source_target_pairs={{0,8},{1,9},{2,10},{3,11},{4,12},{5,13},{6,14},{7,15},{8,0},{9,1},... | collective-permute-start | bytes 614408 | tf_op jit(solution)/shard_map/ppermute | solution.py:712
  388.7 21.6 %collective-permute-start.42 = (bf16[40,2560]{1,0:T(8,128)(2,1)S(1)}, bf16[40,2560]{1,0:T(8,128)(2,1)S(1)}, u32[]{:S(2)}, u32[]{:S(2)}) collective-permute-start(bf16[40,2560]{1,0:T(8,128)(2,1)S(1)} %get-tuple-element.164), channel_id=1, source_target_pairs={{0,4},{1,5},{2,6},{3,7},{4,8},{5,9},{6,10},{7,11},{8,12},{9,13},{1... | collective-permute-start | bytes 614408 | tf_op jit(solution)/shard_map/ppermute | solution.py:712
  391.0 23.2 %collective-permute-start.41 = (bf16[160,2688]{1,0:T(8,128)(2,1)S(1)}, bf16[160,2688]{1,0:T(8,128)(2,1)S(1)}, u32[]{:S(2)}, u32[]{:S(2)}) collective-permute-start(bf16[160,2688]{1,0:T(8,128)(2,1)S(1)} %add_convert_fusion), channel_id=1, source_target_pairs={{0,2},{1,3},{2,0},{3,1},{4,6},{5,7},{6,4},{7,5},{8,10},{9,11},{10,... | collective-permute-start | bytes 2580488 | tf_op jit(solution)/shard_map/ppermute | solution.py:712
  414.4 12.3 %collective-permute-start.47 = (bf16[40,2688]{1,0:T(8,128)(2,1)S(1)}, bf16[40,2688]{1,0:T(8,128)(2,1)S(1)}, u32[]{:S(2)}, u32[]{:S(2)}) collective-permute-start(bf16[40,2688]{1,0:T(8,128)(2,1)S(1)} %get-tuple-element.169), channel_id=1, source_target_pairs={{0,12},{1,13},{2,14},{3,15},{4,0},{5,1},{6,2},{7,3},{8,4},{9,5},{1... | collective-permute-start | bytes 645128 | tf_op jit(solution)/shard_map/ppermute | solution.py:712
  414.5 28.7 %collective-permute-start.46 = (bf16[40,2688]{1,0:T(8,128)(2,1)S(1)}, bf16[40,2688]{1,0:T(8,128)(2,1)S(1)}, u32[]{:S(2)}, u32[]{:S(2)}) collective-permute-start(bf16[40,2688]{1,0:T(8,128)(2,1)S(1)} %get-tuple-element.170), channel_id=1, source_target_pairs={{0,8},{1,9},{2,10},{3,11},{4,12},{5,13},{6,14},{7,15},{8,0},{9,1},... | collective-permute-start | bytes 645128 | tf_op jit(solution)/shard_map/ppermute | solution.py:712
  415.2 28.0 %collective-permute-start.45 = (bf16[40,2688]{1,0:T(8,128)(2,1)S(1)}, bf16[40,2688]{1,0:T(8,128)(2,1)S(1)}, u32[]{:S(2)}, u32[]{:S(2)}) collective-permute-start(bf16[40,2688]{1,0:T(8,128)(2,1)S(1)} %get-tuple-element.171), channel_id=1, source_target_pairs={{0,4},{1,5},{2,6},{3,7},{4,8},{5,9},{6,10},{7,11},{8,12},{9,13},{1... | collective-permute-start | bytes 645128 | tf_op jit(solution)/shard_map/ppermute | solution.py:712
  (53 other events, 827.6 us)
Sparse Core Ops, SparseCore 0:
  10.3 104.7 all-gather.2
  317.8 119.3 reduce-scatter.1

commit v2 on v1

--- a/solution.py
+++ b/solution.py
@@ -170,54 +170,65 @@
         y_ref[...] = acc_ref[...].astype(BF16)
 
 
+def mlp_fwd_skip_body(chunk, rows, flag_ref, c_ref, m_ref, vec_ref, wup_ref, wdown_ref, bup_ref, y_ref, acc_ref):
+    def block(wup, wdown, bup):
+        for r in range(c_ref.shape[0] // rows):
+            at = slice(r * rows, r * rows + rows)
+            act = gelu_pair(dot(c_ref[at], wup[...]) + bup[...])[0].astype(BF16)
+            acc_ref[at] += dot(act, wdown[...])
+
+    @pl.when(flag_ref[0] == 0)
+    def _():
+        width, ff = wup_ref.shape
+        acc_ref[...] = m_ref[...] + vec_ref[7:8]
+        pltpu.emit_pipeline(
+            block,
+            grid=(ff // chunk,),
+            in_specs=[pl.BlockSpec((width, chunk), lambda i: (0, i)), pl.BlockSpec((chunk, width), lambda i: (i, 0)),
+                      pl.BlockSpec((1, chunk), lambda i: (0, i))],
+        )(wup_ref, wdown_ref, bup_ref)
+        y_ref[...] = acc_ref[...].astype(BF16)
+
+
 def mlp_fwd(c, m, wup, wdown, bup, vec, at, parts, flag, after=(), chunk=1280, rows=256):
     n, width = c.shape
     n //= parts
-    ff = wup.shape[1]
-    waits = len(after)
-    part = pl.BlockSpec((n, width), lambda i, flag: (at, 0))
-    here = lambda i, flag: i * (1 - flag[0])
-
-    def body(flag_ref, *refs):
-        @pl.when(flag_ref[0] == 0)
-        def _():
-            mlp_fwd_body(False, rows, *refs[:6], *refs[6 + waits:])
-
-    return pl.pallas_call(
-        body,
-        grid_spec=pltpu.PrefetchScalarGridSpec(
-            num_scalar_prefetch=1,
-            grid=(ff // chunk,),
-            in_specs=[part, part, pl.BlockSpec((width, chunk), lambda i, flag: (0, here(i, flag))),
-                      pl.BlockSpec((chunk, width), lambda i, flag: (here(i, flag), 0)),
-                      pl.BlockSpec((1, chunk), lambda i, flag: (0, here(i, flag))), whole(vec.shape)] + tied(waits),
-            out_specs=whole((n, width)),
-            scratch_shapes=[pltpu.VMEM((n, width), F32)],
-        ),
+    part = pl.BlockSpec((n, width), lambda i: (at, 0))
+    return pl.pallas_call(
+        lambda *refs: mlp_fwd_skip_body(chunk, rows, *refs[:7], *refs[7 + len(after):]),
+        grid=(1,),
+        in_specs=[pl.BlockSpec(memory_space=pltpu.SMEM), part, part, whole(vec.shape)] + tied(3 + len(after)),
+        out_specs=whole((n, width)),
         out_shape=jax.ShapeDtypeStruct((n, width), BF16),
+        scratch_shapes=[pltpu.VMEM((n, width), F32)],
         compiler_params=pltpu.CompilerParams(vmem_limit_bytes=VMEM_LIMIT),
         cost_estimate=cost(13),
         name="feed_forward",
-    )(flag, c, m, wup, wdown, bup, vec, *after)
-
-
-def pre_grad_body(flag_ref, dz_ref, wdown_ref, dg_ref):
+    )(flag, c, m, vec, wup, wdown, bup, *after)
+
+
+def pre_grad_body(chunk, flag_ref, dz_ref, wdown_ref, dg_ref):
+    def block(dz, weights, out):
+        out[...] = dot(dz[...], weights[...], ((1,), (1,))).astype(BF16)
+
     @pl.when(flag_ref[0] > 0)
     def _():
-        dg_ref[...] = dot(dz_ref[...], wdown_ref[...], ((1,), (1,))).astype(BF16)
+        n, width = dz_ref.shape
+        pltpu.emit_pipeline(
+            block,
+            grid=(wdown_ref.shape[0] // chunk,),
+            in_specs=[pl.BlockSpec((n, width), lambda i: (0, 0)), pl.BlockSpec((chunk, width), lambda i: (i, 0))],
+            out_specs=[pl.BlockSpec((n, chunk), lambda i: (0, i))],
+        )(dz_ref, wdown_ref, dg_ref)
 
 
 def pre_grad(dz, wdown, flag, after, chunk=1280):
     n, width = dz.shape
     ff = wdown.shape[0]
     return pl.pallas_call(
-        lambda *refs: pre_grad_body(*refs[:3], *refs[3 + len(after):]),
-        grid_spec=pltpu.PrefetchScalarGridSpec(
-            num_scalar_prefetch=1,
-            grid=(ff // chunk,),
-            in_specs=[pl.BlockSpec(dz.shape, lambda i, flag: (0, 0)), pl.BlockSpec((chunk, width), lambda i, flag: (i * flag[0], 0))] + tied(len(after)),
-            out_specs=pl.BlockSpec((n, chunk), lambda i, flag: (0, i * flag[0])),
-        ),
+        lambda *refs: pre_grad_body(chunk, *refs[:3], *refs[3 + len(after):]),
+        in_specs=[pl.BlockSpec(memory_space=pltpu.SMEM)] + tied(2 + len(after)),
+        out_specs=pl.BlockSpec(memory_space=pl.ANY),
         out_shape=jax.ShapeDtypeStruct((n, ff), BF16),
         compiler_params=pltpu.CompilerParams(vmem_limit_bytes=VMEM_LIMIT),
         cost_estimate=cost(11),

time: 463 us -> 462 us (level)
  transfers between devices with their start and end apart: 50 -> 50, of which waited for: 25 -> 25; matrix products, arithmetic and copies ran while one was open for 5% -> 5% of each run, Pallas kernels for 26% -> 25%
where the time goes in v2:
time: 462 us; the launch traced here: 453 us
  Pallas kernels  217 us (47%)
  waiting for transfers between devices  143 us (31%)
  starting transfers between devices  49.8 us (11%)
  other arithmetic  17.5 us (4%)
  between operations  14.9 us (3%)
  local copies, waits for them, and re-layouts  10.4 us (2%)
    ppermute x44, waiting for transfers between devices, hop(): return lax.ppermute(value, 'dp', pairs)  121 us
    pallas_call x3, Pallas kernels, attn_fwd(): pl.pallas_call(lambda *refs: attn_fwd_body(save, at * count, *refs[:used]...  39.9 us
    ppermute x44, starting transfers between devices, hop(): return lax.ppermute(value, 'dp', pairs)  39.9 us
    pallas_call x3, Pallas kernels, attn_bwd(): pl.pallas_call(body, grid=(count,), in_specs=in_specs, out_specs=specs, o...  38.6 us
    pallas_call x1, Pallas kernels, mlp_both(): pl.pallas_call(lambda *refs: mlp_both_body(rows, *refs), grid=(ff // chun...  37.3 us
    pallas_call x1, Pallas kernels, mlp_grad(): pl.pallas_call(lambda *refs: mlp_grad_body(rows, *refs[:7], *refs[7 + wai...  22.4 us
    ppermute x2, waiting for transfers between devices, on_device(): arrived.append(lax.ppermute(back, 'section', [(1, 0)]))  19.2 us
    pallas_call x1, Pallas kernels, mlp_fwd(): pl.pallas_call(lambda *refs: mlp_fwd_skip_body(chunk, rows, *refs[:7], *r...  13.6 us
  transfers between devices with their start and end apart: 50, of which 25 were waited for; matrix products, arithmetic and copies ran while one was open for 5% of the time, Pallas kernels for 25%

profile of v2, /device:TPU:0, one launch (start us, length us, event | category | flops | bytes accessed | tf_op | source)
XLA Modules:
  0.0 453.1 jit_solution(1311711781912514516)
XLA Ops:
  10.6 3.0 collective-permute-start.2
  13.7 3.6 collective-permute-start.1
  19.0 5.1 %collective-permute-done.1.refs_4_ = bf16[40,2688]{1,0:T(8,128)(2,1)S(1)} collective-permute-done((bf16[40,2688]{1,0:T(8,128)(2,1)S(1)}, bf16[40,2688]{1,0:T(8,128)(2,1)S(1)}, u32[]{:S(2)}, u32[]{:S(2)}) %collective-permute-start.1) | collective-permute-done | bytes 215072 | tf_op jit(solution)/shard_map/ppermute | solution.py:723
  24.1 8.2 %collective-permute-done.refs_2_ = bf16[40,2688]{1,0:T(8,128)(2,1)S(1)} collective-permute-done((bf16[40,2688]{1,0:T(8,128)(2,1)S(1)}, bf16[40,2688]{1,0:T(8,128)(2,1)S(1)}, u32[]{:S(2)}, u32[]{:S(2)}) %collective-permute-start) | collective-permute-done | bytes 215072 | tf_op jit(solution)/shard_map/ppermute | solution.py:723
  34.8 3.5 collective-permute-start.3
  40.3 18.0 %collective-permute-done.3.refs_3_ = bf16[40,2688]{1,0:T(8,128)(2,1)S(1)} collective-permute-done((bf16[40,2688]{1,0:T(8,128)(2,1)S(1)}, bf16[40,2688]{1,0:T(8,128)(2,1)S(1)}, u32[]{:S(2)}, u32[]{:S(2)}) %collective-permute-start.3) | collective-permute-done | bytes 215072 | tf_op jit(solution)/shard_map/ppermute | solution.py:723
  62.0 8.8 %collective-permute-done.8.refs_7_ = bf16[40,2688]{1,0:T(8,128)(2,1)} collective-permute-done((bf16[40,2688]{1,0:T(8,128)(2,1)S(1)}, bf16[40,2688]{1,0:T(8,128)(2,1)}, u32[]{:S(2)}, u32[]{:S(2)}) %collective-permute-start.8) | collective-permute-done | bytes 215072 | tf_op jit(solution)/shard_map/ppermute | solution.py:723
  71.2 13.9 %collective-permute-done.17.refs_7_ = bf16[320,640]{1,0:T(8,128)(2,1)S(1)} collective-permute-done((bf16[320,640]{1,0:T(8,128)(2,1)}, bf16[320,640]{1,0:T(8,128)(2,1)S(1)}, u32[]{:S(2)}, u32[]{:S(2)}) %collective-permute-start.17) | collective-permute-done | bytes 409632 | tf_op jit(solution)/shard_map/ppermute | solution.py:723
  91.2 5.0 %place_pieces.1 = bf16[16,40,2688]{2,1,0:T(8,128)(2,1)} custom-call(s32[16]{0:T(128)} %stack.67.refs_0_, bf16[40,2688]{1,0:T(8,128)(2,1)} %copy-done.8, bf16[40,2688]{1,0:T(8,128)(2,1)} %copy-done.27, bf16[40,2688]{1,0:T(8,128)(2,1)} %copy-done.28, bf16[40,2688]{1,0:T(8,128)(2,1)} %copy-done.26, bf16[40,2688]{1,0:T(8,128)(2,1)} %copy-done.25, ...), custom_call_target="tpu_custom_call" | custom-call | flops 4400000000 | bytes 1024 | tf_op jit(solution)/shard_map/place_pieces/pallas_call | solution.py:627
  98.8 16.7 %attention_forward.3 = (f32[4,256,640]{2,1,0:T(8,128)}, bf16[4,256,640]{2,1,0:T(8,128)(2,1)}) custom-call(s32[5]{0:T(128)} %pad_add_fusion.refs_0_, bf16[4,256,640]{2,1,0:T(8,128)(2,1)} %refs_1_.7, bf16[640,2688]{1,0:T(8,128)(2,1)} %bitcast.57, f32[8,640]{1,0:T(8,128)} %convert_bitcast_fusion.refs_3_.refs_4_.refs_6_.refs_9_, ...), custom_call_target="tpu_custom_call" | custom-call | flops 19800000512 | bytes 1024 | tf_op jit(solution)/shard_map/attention_forward/pallas_call | solution.py:131
  119.3 8.6 %feed_forward_up.1.refs_1_ = bf16[512,5120]{1,0:T(8,128)(2,1)} custom-call(bf16[1024,640]{1,0:T(8,128)(2,1)} %bitcast.89, bf16[640,5120]{1,0:T(8,128)(2,1)} %bitcast.67, f32[1,5120]{1,0:T(1,128)} %reshape.201.refs_4_.refs_2_.refs_6_.refs_5_), custom_call_target="tpu_custom_call" | custom-call | flops 7040000000 | bytes 1024 | tf_op jit(solution)/shard_map/feed_forward_up/pallas_call | solution.py:292
  134.5 11.0 %place_and_feed_forward_down.1 = (bf16[5120,640]{1,0:T(8,128)(2,1)}, bf16[512,640]{1,0:T(8,128)(2,1)}) custom-call(s32[16]{0:T(128)} %stack.67.refs_0_, bf16[512,5120]{1,0:T(8,128)(2,1)} %feed_forward_up.1.refs_1_, f32[1024,640]{1,0:T(8,128)} %bitcast.82, f32[8,640]{1,0:T(8,128)} %convert_bitcast_fusion.refs_3_.refs_4_.refs_6_.refs_9_, ...), custom_call_target="tpu_custom_call" | custom-call | flops 11000000512 | bytes 1024 | tf_op jit(solution)/shard_map/place_and_feed_forward_down/pallas_call | solution.py:661
  145.6 3.7 collective-permute-start.31
  149.5 13.6 %feed_forward.1 = bf16[512,640]{1,0:T(8,128)(2,1)} custom-call(s32[1]{0:T(128)} %bitcast.refs_0_.refs_10_, bf16[1024,640]{1,0:T(8,128)(2,1)} %bitcast.90, f32[1024,640]{1,0:T(8,128)} %bitcast.83, f32[8,640]{1,0:T(8,128)} %convert_bitcast_fusion.refs_3_.refs_4_.refs_6_.refs_9_, bf16[640,5120]{1,0:T(8,128)(2,1)} %bitcast.68, ...), custom_call_target="tpu_custom_call" | custom-call | flops 14300000256 | bytes 1024 | tf_op jit(solution)/shard_map/feed_forward/pallas_call | solution.py:197
  163.1 3.5 collective-permute-start.30
  167.4 11.6 %attention_forward.4 = (f32[4,256,640]{2,1,0:T(8,128)}, bf16[4,256,640]{2,1,0:T(8,128)(2,1)}, bf16[4,256,1920]{2,1,0:T(8,128)(2,1)}, bf16[4,20,256,256]{3,2,1,0:...) custom-call(s32[5]{0:T(128)} %pad_add_fusion.refs_0_, ...), custom_call_target="tpu_custom_call" | custom-call | flops 9900000256 | bytes 1024 | tf_op jit(solution)/shard_map/attention_forward/pallas_call | solution.py:131
  182.1 11.6 %attention_forward.5 = (f32[4,256,640]{2,1,0:T(8,128)}, bf16[4,256,640]{2,1,0:T(8,128)(2,1)}, bf16[4,256,1920]{2,1,0:T(8,128)(2,1)}, bf16[4,20,256,256]{3,2,1,0:...) custom-call(s32[5]{0:T(128)} %pad_add_fusion.refs_0_, ...), custom_call_target="tpu_custom_call", output_to_operand_aliasing={{0}: (5, {}), {1}: (6, {}), {2}: (7, {}), {3}: (8, {}), {4}... | custom-call | flops 9900000256 | bytes 1024 | tf_op jit(solution)/shard_map/attention_forward/pallas_call | solution.py:131
  193.8 37.3 %feed_forward_both.1 = (bf16[1024,640]{1,0:T(8,128)(2,1)}, bf16[1024,5120]{1,0:T(8,128)(2,1)}, bf16[1024,5120]{1,0:T(8,128)(2,1)}, f32[1024,640]{1,0:T(8,128)}) custom-call(bf16[1024,640]{1,0:T(8,128)(2,1)} %bitcast.92, f32[1024,640]{1,0:T(8,128)} %bitcast.84, bf16[1024,5120]{1,0:T(8,128)(2,1)} %feed_forward_early_gradient.1.refs_7_.refs_2_, ...), custom_call_target="tpu_custom_call" | custom-call | flops 39600001024 | bytes 1024 | tf_op jit(solution)/shard_map/feed_forward_both/pallas_call | solution.py:266
  231.1 6.5 %attention_back.4 = bf16[2,256,640]{2,1,0:T(8,128)(2,1)} custom-call(f32[4,256,640]{2,1,0:T(8,128)} %bitcast.86, bf16[4,256,640]{2,1,0:T(8,128)(2,1)} %refs_1_.9, f32[4,256,640]{2,1,0:T(8,128)} %get-tuple-element.126.refs_2_, bf16[4,256,640]{2,1,0:T(8,128)(2,1)} %get-tuple-element.129.refs_3_, bf16[4,256,1920]{2,1,0:T(8,128)(2,1)} %get-tuple-element.130.refs_4_, ...), custom_call_target="tpu_custom_call" | custom-call | flops 15399999488 | bytes 1024 | tf_op jit(solution)/shard_map/attention_back/pallas_call | solution.py:564
  239.0 6.7 %attention_back.3 = bf16[2,256,640]{2,1,0:T(8,128)(2,1)} custom-call(f32[4,256,640]{2,1,0:T(8,128)} %bitcast.87, bf16[4,256,640]{2,1,0:T(8,128)(2,1)} %refs_1_.9, f32[4,256,640]{2,1,0:T(8,128)} %get-tuple-element.126.refs_2_, bf16[4,256,640]{2,1,0:T(8,128)(2,1)} %get-tuple-element.129.refs_3_, bf16[4,256,1920]{2,1,0:T(8,128)(2,1)} %get-tuple-element.130.refs_4_, ...), custom_call_target="tpu_custom_call" | custom-call | flops 15399999488 | bytes 1024 | tf_op jit(solution)/shard_map/attention_back/pallas_call | solution.py:564
  246.9 17.3 %collective-permute-done.33 = bf16[2,256,640]{2,1,0:T(8,128)(2,1)S(1)} collective-permute-done((bf16[2,256,640]{2,1,0:T(8,128)(2,1)}, bf16[2,256,640]{2,1,0:T(8,128)(2,1)S(1)}, u32[]{:S(2)}, u32[]{:S(2)}) %collective-permute-start.33) | collective-permute-done | bytes 655392 | tf_op jit(solution)/shard_map/ppermute | solution.py:854
  265.1 13.4 %feed_forward_back.1 = (f32[1024,640]{1,0:T(8,128)}, bf16[512,5120]{1,0:T(8,128)(2,1)}) custom-call(bf16[512,640]{1,0:T(8,128)(2,1)} %bitcast.50, bf16[1024,5120]{1,0:T(8,128)(2,1)} %get-tuple-element.134.refs_1_, bf16[640,5120]{1,0:T(8,128)(2,1)} %bitcast.70, bf16[5120,640]{1,0:T(8,128)(2,1)} %get-tuple-element.114.refs_2_.refs_5_.refs_4_.refs_3_), custom_call_target="tpu_custom_call" | custom-call | flops 12099999744 | bytes 1024 | tf_op jit(solution)/shard_map/feed_forward_back/pallas_call | solution.py:359
  281.8 12.4 %down_gradient.1.refs_8_ = bf16[5120,640]{1,0:T(8,128)(2,1)} custom-call(bf16[1024,5120]{1,0:T(8,128)(2,1)} %get-tuple-element.138.refs_0_, bf16[1024,640]{1,0:T(8,128)(2,1)} %bitcast.52), custom_call_target="tpu_custom_call" | custom-call | flops 13200000000 | bytes 1024 | tf_op jit(solution)/shard_map/down_gradient/pallas_call | solution.py:457
  294.2 22.4 %feed_forward_gradients.1 = (f32[1024,640]{1,0:T(8,128)}, bf16[320,5120]{1,0:T(8,128)(2,1)}, bf16[320,5120]{1,0:T(8,128)(2,1)}, f32[8,5120]{1,0:T(8,128)}) custom-call(bf16[512,640]{1,0:T(8,128)(2,1)} %bitcast.49, bf16[1024,5120]{1,0:T(8,128)(2,1)} %get-tuple-element.134.refs_1_, bf16[640,5120]{1,0:T(8,128)(2,1)} %bitcast.71, ...), custom_call_target="tpu_custom_call", output_to_operand_aliasing={{0}: (7, {})} | custom-call | flops 23100000256 | bytes 1024 | tf_op jit(solution)/shard_map/feed_forward_gradients/pallas_call | solution.py:434
  327.8 25.5 %attention_back.5 = (f32[4,256,640]{2,1,0:T(8,128)}, bf16[4,256,640]{2,1,0:T(8,128)(2,1)}, bf16[4,256,1920]{2,1,0:T(8,128)(2,1)}, f32[8,640]{1,0:T(8,128)}) custom-call(f32[4,256,640]{2,1,0:T(8,128)} %bitcast.85, bf16[4,256,640]{2,1,0:T(8,128)(2,1)} %pad_maximum_fusion.refs_1_, f32[4,256,640]{2,1,0:T(8,128)} %get-tuple-element.126.refs_2_, ...), custom_call_target="tpu_custom_call" | custom-call | flops 30799998976 | bytes 1024 | tf_op jit(solution)/shard_map/attention_back/pallas_call | solution.py:564
  357.1 11.7 %projection_gradients.1 = (bf16[320,2688]{1,0:T(8,128)(2,1)}, bf16[320,2688]{1,0:T(8,128)(2,1)}) custom-call(bf16[1024,640]{1,0:T(8,128)(2,1)} %bitcast.95, bf16[1024,1920]{1,0:T(8,128)(2,1)} %bitcast.80, bf16[1024,640]{1,0:T(8,128)(2,1)} %bitcast.94, bf16[1024,640]{1,0:T(8,128)(2,1)} %bitcast.91, f32[8,640]{1,0:T(8,128)} %get-tuple-element.145.refs_4_, ...), custom_call_target="tpu_custom_call" | custom-call | flops 9900000256 | bytes 1024 | tf_op jit(solution)/shard_map/projection_gradients/pallas_call | solution.py:601
  368.8 9.6 %collective-permute-done.36 = bf16[160,2560]{1,0:T(8,128)(2,1)S(1)} collective-permute-done((bf16[160,2560]{1,0:T(8,128)(2,1)S(1)}, bf16[160,2560]{1,0:T(8,128)(2,1)S(1)}, u32[]{:S(2)}, u32[]{:S(2)}) %collective-permute-start.36) | collective-permute-done | bytes 819232 | tf_op jit(solution)/shard_map/ppermute | solution.py:723
  382.4 5.4 %collective-permute-start.43 = (bf16[40,2560]{1,0:T(8,128)(2,1)S(1)}, bf16[40,2560]{1,0:T(8,128)(2,1)S(1)}, u32[]{:S(2)}, u32[]{:S(2)}) collective-permute-start(bf16[40,2560]{1,0:T(8,128)(2,1)S(1)} %get-tuple-element.163), channel_id=1, source_target_pairs={{0,8},{1,9},{2,10},{3,11},{4,12},{5,13},{6,14},{7,15},{8,0},{9,1},... | collective-permute-start | bytes 614408 | tf_op jit(solution)/shard_map/ppermute | solution.py:723
  390.6 5.2 %collective-permute-done.44 = bf16[40,2560]{1,0:T(8,128)(2,1)S(1)} collective-permute-done((bf16[40,2560]{1,0:T(8,128)(2,1)S(1)}, bf16[40,2560]{1,0:T(8,128)(2,1)S(1)}, u32[]{:S(2)}, u32[]{:S(2)}) %collective-permute-start.44) | collective-permute-done | bytes 204832 | tf_op jit(solution)/shard_map/ppermute | solution.py:723
  395.9 13.5 %collective-permute-done.43 = bf16[40,2560]{1,0:T(8,128)(2,1)S(1)} collective-permute-done((bf16[40,2560]{1,0:T(8,128)(2,1)S(1)}, bf16[40,2560]{1,0:T(8,128)(2,1)S(1)}, u32[]{:S(2)}, u32[]{:S(2)}) %collective-permute-start.43) | collective-permute-done | bytes 204832 | tf_op jit(solution)/shard_map/ppermute | solution.py:723
  417.8 8.6 %collective-permute-done.47.refs_5_ = bf16[40,2688]{1,0:T(8,128)(2,1)S(1)} collective-permute-done((bf16[40,2688]{1,0:T(8,128)(2,1)S(1)}, bf16[40,2688]{1,0:T(8,128)(2,1)S(1)}, u32[]{:S(2)}, u32[]{:S(2)}) %collective-permute-start.47) | collective-permute-done | bytes 215072 | tf_op jit(solution)/shard_map/ppermute | solution.py:723
  426.4 15.8 %collective-permute-done.46.refs_4_ = bf16[40,2688]{1,0:T(8,128)(2,1)S(1)} collective-permute-done((bf16[40,2688]{1,0:T(8,128)(2,1)S(1)}, bf16[40,2688]{1,0:T(8,128)(2,1)S(1)}, u32[]{:S(2)}, u32[]{:S(2)}) %collective-permute-start.46) | collective-permute-done | bytes 215072 | tf_op jit(solution)/shard_map/ppermute | solution.py:723
  (185 shorter events, 77.7 us)
Async XLA Ops:
  7.2 112.1 %all-gather.3.cloned.1.call-start = ((), (), s32[]{:S(2)}) async-start(), calls=%async_computation.2 | async-start | bytes 6963200 | tf_op jit(solution)/shard_map/all_gather | solution.py:804
  7.9 434.3 %reduce-scatter.2.cloned.1.call-start = ((), (), s32[]{:S(2)}) async-start(), calls=%async_computation.1 | async-start | bytes 6963200 | tf_op jit(solution)/shard_map/reduce_scatter | solution.py:861
  17.3 15.0 %collective-permute-start = (bf16[40,2688]{1,0:T(8,128)(2,1)S(1)}, bf16[40,2688]{1,0:T(8,128)(2,1)S(1)}, u32[]{:S(2)}, u32[]{:S(2)}) collective-permute-start(bf16[40,2688]{1,0:T(8,128)(2,1)S(1)} %pad_maximum_fusion.1.refs_1_), channel_id=1, source_target_pairs={{0,4},{1,5},{2,6},{3,7},{4,8},{5,9},{6,10},{7,11},{8,12},{9,13},{1... | collective-permute-start | bytes 645128 | tf_op jit(solution)/shard_map/ppermute | solution.py:723
  17.3 23.0 %collective-permute-start.6 = (bf16[320,640]{1,0:T(8,128)(2,1)}, bf16[320,640]{1,0:T(8,128)(2,1)S(1)}, u32[]{:S(2)}, u32[]{:S(2)}) collective-permute-start(bf16[320,640]{1,0:T(8,128)(2,1)} %bitcast.74), channel_id=1, source_target_pairs={{0,2},{1,3},{2,0},{3,1},{4,6},{5,7},{6,4},{7,5},{8,10},{9,11},{10,... | collective-permute-start | bytes 1228808 | tf_op jit(solution)/shard_map/ppermute | solution.py:723
  32.3 26.0 %collective-permute-start.7 = (bf16[320,640]{1,0:T(8,128)(2,1)}, bf16[320,640]{1,0:T(8,128)(2,1)S(1)}, u32[]{:S(2)}, u32[]{:S(2)}) collective-permute-start(bf16[320,640]{1,0:T(8,128)(2,1)} %bitcast.75), channel_id=1, source_target_pairs={{0,4},{1,5},{2,6},{3,7},{4,8},{5,9},{6,10},{7,11},{8,12},{9,13},{1... | collective-permute-start | bytes 1228808 | tf_op jit(solution)/shard_map/ppermute | solution.py:723
  34.8 23.5 %collective-permute-start.3 = (bf16[40,2688]{1,0:T(8,128)(2,1)S(1)}, bf16[40,2688]{1,0:T(8,128)(2,1)S(1)}, u32[]{:S(2)}, u32[]{:S(2)}) collective-permute-start(bf16[40,2688]{1,0:T(8,128)(2,1)S(1)} %pad_maximum_fusion.1.refs_1_), channel_id=1, source_target_pairs={{0,8},{1,9},{2,10},{3,11},{4,12},{5,13},{6,14},{7,15},{8,0},{9,1},... | collective-permute-start | bytes 645128 | tf_op jit(solution)/shard_map/ppermute | solution.py:723
  38.2 20.0 %collective-permute-start.4 = (bf16[40,2688]{1,0:T(8,128)(2,1)S(1)}, bf16[40,2688]{1,0:T(8,128)(2,1)}, u32[]{:S(2)}, u32[]{:S(2)}) collective-permute-start(bf16[40,2688]{1,0:T(8,128)(2,1)S(1)} %collective-permute-done.refs_2_), channel_id=1, source_target_pairs={{0,2},{1,3},{2,0},{3,1},{4,6},{5,7},{6,4},{7,5},{8,10},{9,11},{10,... | collective-permute-start | bytes 645128 | tf_op jit(solution)/shard_map/ppermute | solution.py:723
  38.2 20.0 %collective-permute-start.5 = (bf16[40,2688]{1,0:T(8,128)(2,1)S(1)}, bf16[40,2688]{1,0:T(8,128)(2,1)}, u32[]{:S(2)}, u32[]{:S(2)}) collective-permute-start(bf16[40,2688]{1,0:T(8,128)(2,1)S(1)} %collective-permute-done.1.refs_4_), channel_id=1, source_target_pairs={{0,2},{1,3},{2,0},{3,1},{4,6},{5,7},{6,4},{7,5},{8,10},{9,11},{10,... | collective-permute-start | bytes 645128 | tf_op jit(solution)/shard_map/ppermute | solution.py:723
  58.3 12.4 %collective-permute-start.8 = (bf16[40,2688]{1,0:T(8,128)(2,1)S(1)}, bf16[40,2688]{1,0:T(8,128)(2,1)}, u32[]{:S(2)}, u32[]{:S(2)}) collective-permute-start(bf16[40,2688]{1,0:T(8,128)(2,1)S(1)} %collective-permute-done.3.refs_3_), channel_id=1, source_target_pairs={{0,2},{1,3},{2,0},{3,1},{4,6},{5,7},{6,4},{7,5},{8,10},{9,11},{10,... | collective-permute-start | bytes 645128 | tf_op jit(solution)/shard_map/ppermute | solution.py:723
  58.9 26.2 %collective-permute-start.17 = (bf16[320,640]{1,0:T(8,128)(2,1)}, bf16[320,640]{1,0:T(8,128)(2,1)S(1)}, u32[]{:S(2)}, u32[]{:S(2)}) collective-permute-start(bf16[320,640]{1,0:T(8,128)(2,1)} %bitcast.76), channel_id=1, source_target_pairs={{0,12},{1,13},{2,14},{3,15},{4,0},{5,1},{6,2},{7,3},{8,4},{9,5},{1... | collective-permute-start | bytes 1228808 | tf_op jit(solution)/shard_map/ppermute | solution.py:723
  60.4 26.1 %collective-permute-start.18 = (bf16[320,640]{1,0:T(8,128)(2,1)S(1)}, bf16[320,640]{1,0:T(8,128)(2,1)S(1)}, u32[]{:S(2)}, u32[]{:S(2)}) collective-permute-start(bf16[320,640]{1,0:T(8,128)(2,1)S(1)} %collective-permute-done.7.refs_5_), channel_id=1, source_target_pairs={{0,2},{1,3},{2,0},{3,1},{4,6},{5,7},{6,4},{7,5},{8,10},{9,11},{10,... | collective-permute-start | bytes 1228808 | tf_op jit(solution)/shard_map/ppermute | solution.py:723
  70.7 15.8 %collective-permute-start.9 = (bf16[40,2688]{1,0:T(8,128)(2,1)S(1)}, bf16[40,2688]{1,0:T(8,128)(2,1)S(1)}, u32[]{:S(2)}, u32[]{:S(2)}) collective-permute-start(bf16[40,2688]{1,0:T(8,128)(2,1)S(1)} %pad_maximum_fusion.1.refs_1_), channel_id=1, source_target_pairs={{0,1},{1,0},{2,3},{3,2},{4,5},{5,4},{6,7},{7,6},{8,9},{9,8},{10,11... | collective-permute-start | bytes 645128 | tf_op jit(solution)/shard_map/ppermute | solution.py:723
  70.7 16.3 %collective-permute-start.10 = (bf16[40,2688]{1,0:T(8,128)(2,1)S(1)}, bf16[40,2688]{1,0:T(8,128)(2,1)S(1)}, u32[]{:S(2)}, u32[]{:S(2)}) collective-permute-start(bf16[40,2688]{1,0:T(8,128)(2,1)S(1)} %collective-permute-done.refs_2_), channel_id=1, source_target_pairs={{0,1},{1,0},{2,3},{3,2},{4,5},{5,4},{6,7},{7,6},{8,9},{9,8},{10,11... | collective-permute-start | bytes 645128 | tf_op jit(solution)/shard_map/ppermute | solution.py:723
  71.2 15.9 %collective-permute-start.11 = (bf16[40,2688]{1,0:T(8,128)(2,1)S(1)}, bf16[40,2688]{1,0:T(8,128)(2,1)S(1)}, u32[]{:S(2)}, u32[]{:S(2)}) collective-permute-start(bf16[40,2688]{1,0:T(8,128)(2,1)S(1)} %collective-permute-done.3.refs_3_), channel_id=1, source_target_pairs={{0,1},{1,0},{2,3},{3,2},{4,5},{5,4},{6,7},{7,6},{8,9},{9,8},{10,11... | collective-permute-start | bytes 645128 | tf_op jit(solution)/shard_map/ppermute | solution.py:723
  90.1 27.5 %collective-permute-start.19 = (bf16[320,640]{1,0:T(8,128)(2,1)}, bf16[320,640]{1,0:T(8,128)(2,1)S(1)}, u32[]{:S(2)}, u32[]{:S(2)}) collective-permute-start(bf16[320,640]{1,0:T(8,128)(2,1)} %bitcast.77), channel_id=1, source_target_pairs={{0,8},{1,9},{2,10},{3,11},{4,12},{5,13},{6,14},{7,15},{8,0},{9,1},... | collective-permute-start | bytes 1228808 | tf_op jit(solution)/shard_map/ppermute | solution.py:723
  90.2 27.4 %collective-permute-start.20 = (bf16[320,640]{1,0:T(8,128)(2,1)S(1)}, bf16[320,640]{1,0:T(8,128)(2,1)S(1)}, u32[]{:S(2)}, u32[]{:S(2)}) collective-permute-start(bf16[320,640]{1,0:T(8,128)(2,1)S(1)} %collective-permute-done.17.refs_7_), channel_id=1, source_target_pairs={{0,2},{1,3},{2,0},{3,1},{4,6},{5,7},{6,4},{7,5},{8,10},{9,11},{10,... | collective-permute-start | bytes 1228808 | tf_op jit(solution)/shard_map/ppermute | solution.py:723
  145.6 21.0 %collective-permute-start.31 = (bf16[2,256,640]{2,1,0:T(8,128)(2,1)}, bf16[2,256,640]{2,1,0:T(8,128)(2,1)S(1)}, u32[]{:S(2)}, u32[]{:S(2)}) collective-permute-start(bf16[2,256,640]{2,1,0:T(8,128)(2,1)} %bitcast.72), channel_id=1, source_target_pairs={{0,16},{1,17},{2,18},{3,19},{4,20},{5,21},{6,22},{7,23},{8,24},{9,... | collective-permute-start | bytes 1966088 | tf_op jit(solution)/shard_map/ppermute | solution.py:844
  163.1 18.2 %collective-permute-start.30 = (bf16[2,256,640]{2,1,0:T(8,128)(2,1)}, bf16[2,256,640]{2,1,0:T(8,128)(2,1)S(1)}, u32[]{:S(2)}, u32[]{:S(2)}) collective-permute-start(bf16[2,256,640]{2,1,0:T(8,128)(2,1)} %bitcast.73), channel_id=1, source_target_pairs={{0,16},{1,17},{2,18},{3,19},{4,20},{5,21},{6,22},{7,23},{8,24},{9,... | collective-permute-start | bytes 1966088 | tf_op jit(solution)/shard_map/ppermute | solution.py:844
  237.5 26.6 %collective-permute-start.33 = (bf16[2,256,640]{2,1,0:T(8,128)(2,1)}, bf16[2,256,640]{2,1,0:T(8,128)(2,1)S(1)}, u32[]{:S(2)}, u32[]{:S(2)}) collective-permute-start(bf16[2,256,640]{2,1,0:T(8,128)(2,1)} %attention_back.4), channel_id=1, source_target_pairs={{16,0},{17,1},{18,2},{19,3},{20,4},{21,5},{22,6},{23,7},{24,8},{25... | collective-permute-start | bytes 1966088 | tf_op jit(solution)/shard_map/ppermute | solution.py:854
  245.6 34.8 %collective-permute-start.32 = (bf16[2,256,640]{2,1,0:T(8,128)(2,1)}, bf16[2,256,640]{2,1,0:T(8,128)(2,1)S(1)}, u32[]{:S(2)}, u32[]{:S(2)}) collective-permute-start(bf16[2,256,640]{2,1,0:T(8,128)(2,1)} %attention_back.3), channel_id=1, source_target_pairs={{16,0},{17,1},{18,2},{19,3},{20,4},{21,5},{22,6},{23,7},{24,8},{25... | collective-permute-start | bytes 1966088 | tf_op jit(solution)/shard_map/ppermute | solution.py:854
  324.3 29.0 %collective-permute-start.35 = (bf16[160,2560]{1,0:T(8,128)(2,1)S(1)}, bf16[160,2560]{1,0:T(8,128)(2,1)S(1)}, u32[]{:S(2)}, u32[]{:S(2)}) collective-permute-start(bf16[160,2560]{1,0:T(8,128)(2,1)S(1)} %add_convert_fusion.2), channel_id=1, source_target_pairs={{0,2},{1,3},{2,0},{3,1},{4,6},{5,7},{6,4},{7,5},{8,10},{9,11},{10,... | collective-permute-start | bytes 2457608 | tf_op jit(solution)/shard_map/ppermute | solution.py:723
  326.5 51.9 %collective-permute-start.36 = (bf16[160,2560]{1,0:T(8,128)(2,1)S(1)}, bf16[160,2560]{1,0:T(8,128)(2,1)S(1)}, u32[]{:S(2)}, u32[]{:S(2)}) collective-permute-start(bf16[160,2560]{1,0:T(8,128)(2,1)S(1)} %add_convert_fusion.1), channel_id=1, source_target_pairs={{0,2},{1,3},{2,0},{3,1},{4,6},{5,7},{6,4},{7,5},{8,10},{9,11},{10,... | collective-permute-start | bytes 2457608 | tf_op jit(solution)/shard_map/ppermute | solution.py:723
  355.0 23.4 %collective-permute-start.39 = (bf16[40,2560]{1,0:T(8,128)(2,1)S(1)}, bf16[40,2560]{1,0:T(8,128)(2,1)S(1)}, u32[]{:S(2)}, u32[]{:S(2)}) collective-permute-start(bf16[40,2560]{1,0:T(8,128)(2,1)S(1)} %get-tuple-element.165), channel_id=1, source_target_pairs={{0,12},{1,13},{2,14},{3,15},{4,0},{5,1},{6,2},{7,3},{8,4},{9,5},{1... | collective-permute-start | bytes 614408 | tf_op jit(solution)/shard_map/ppermute | solution.py:723
  356.2 24.4 %collective-permute-start.38 = (bf16[40,2560]{1,0:T(8,128)(2,1)S(1)}, bf16[40,2560]{1,0:T(8,128)(2,1)S(1)}, u32[]{:S(2)}, u32[]{:S(2)}) collective-permute-start(bf16[40,2560]{1,0:T(8,128)(2,1)S(1)} %get-tuple-element.166), channel_id=1, source_target_pairs={{0,8},{1,9},{2,10},{3,11},{4,12},{5,13},{6,14},{7,15},{8,0},{9,1},... | collective-permute-start | bytes 614408 | tf_op jit(solution)/shard_map/ppermute | solution.py:723
  356.2 24.4 %collective-permute-start.37 = (bf16[40,2560]{1,0:T(8,128)(2,1)S(1)}, bf16[40,2560]{1,0:T(8,128)(2,1)S(1)}, u32[]{:S(2)}, u32[]{:S(2)}) collective-permute-start(bf16[40,2560]{1,0:T(8,128)(2,1)S(1)} %get-tuple-element.167), channel_id=1, source_target_pairs={{0,4},{1,5},{2,6},{3,7},{4,8},{5,9},{6,10},{7,11},{8,12},{9,13},{1... | collective-permute-start | bytes 614408 | tf_op jit(solution)/shard_map/ppermute | solution.py:723
  382.4 13.5 %collective-permute-start.44 = (bf16[40,2560]{1,0:T(8,128)(2,1)S(1)}, bf16[40,2560]{1,0:T(8,128)(2,1)S(1)}, u32[]{:S(2)}, u32[]{:S(2)}) collective-permute-start(bf16[40,2560]{1,0:T(8,128)(2,1)S(1)} %get-tuple-element.162), channel_id=1, source_target_pairs={{0,12},{1,13},{2,14},{3,15},{4,0},{5,1},{6,2},{7,3},{8,4},{9,5},{1... | collective-permute-start | bytes 614408 | tf_op jit(solution)/shard_map/ppermute | solution.py:723
  382.4 27.0 %collective-permute-start.43 = (bf16[40,2560]{1,0:T(8,128)(2,1)S(1)}, bf16[40,2560]{1,0:T(8,128)(2,1)S(1)}, u32[]{:S(2)}, u32[]{:S(2)}) collective-permute-start(bf16[40,2560]{1,0:T(8,128)(2,1)S(1)} %get-tuple-element.163), channel_id=1, source_target_pairs={{0,8},{1,9},{2,10},{3,11},{4,12},{5,13},{6,14},{7,15},{8,0},{9,1},... | collective-permute-start | bytes 614408 | tf_op jit(solution)/shard_map/ppermute | solution.py:723
  387.9 21.6 %collective-permute-start.42 = (bf16[40,2560]{1,0:T(8,128)(2,1)S(1)}, bf16[40,2560]{1,0:T(8,128)(2,1)S(1)}, u32[]{:S(2)}, u32[]{:S(2)}) collective-permute-start(bf16[40,2560]{1,0:T(8,128)(2,1)S(1)} %get-tuple-element.164), channel_id=1, source_target_pairs={{0,4},{1,5},{2,6},{3,7},{4,8},{5,9},{6,10},{7,11},{8,12},{9,13},{1... | collective-permute-start | bytes 614408 | tf_op jit(solution)/shard_map/ppermute | solution.py:723
  390.1 23.4 %collective-permute-start.41 = (bf16[160,2688]{1,0:T(8,128)(2,1)S(1)}, bf16[160,2688]{1,0:T(8,128)(2,1)S(1)}, u32[]{:S(2)}, u32[]{:S(2)}) collective-permute-start(bf16[160,2688]{1,0:T(8,128)(2,1)S(1)} %add_convert_fusion), channel_id=1, source_target_pairs={{0,2},{1,3},{2,0},{3,1},{4,6},{5,7},{6,4},{7,5},{8,10},{9,11},{10,... | collective-permute-start | bytes 2580488 | tf_op jit(solution)/shard_map/ppermute | solution.py:723
  413.7 12.7 %collective-permute-start.47 = (bf16[40,2688]{1,0:T(8,128)(2,1)S(1)}, bf16[40,2688]{1,0:T(8,128)(2,1)S(1)}, u32[]{:S(2)}, u32[]{:S(2)}) collective-permute-start(bf16[40,2688]{1,0:T(8,128)(2,1)S(1)} %get-tuple-element.169), channel_id=1, source_target_pairs={{0,12},{1,13},{2,14},{3,15},{4,0},{5,1},{6,2},{7,3},{8,4},{9,5},{1... | collective-permute-start | bytes 645128 | tf_op jit(solution)/shard_map/ppermute | solution.py:723
  413.8 28.4 %collective-permute-start.46 = (bf16[40,2688]{1,0:T(8,128)(2,1)S(1)}, bf16[40,2688]{1,0:T(8,128)(2,1)S(1)}, u32[]{:S(2)}, u32[]{:S(2)}) collective-permute-start(bf16[40,2688]{1,0:T(8,128)(2,1)S(1)} %get-tuple-element.170), channel_id=1, source_target_pairs={{0,8},{1,9},{2,10},{3,11},{4,12},{5,13},{6,14},{7,15},{8,0},{9,1},... | collective-permute-start | bytes 645128 | tf_op jit(solution)/shard_map/ppermute | solution.py:723
  414.9 27.3 %collective-permute-start.45 = (bf16[40,2688]{1,0:T(8,128)(2,1)S(1)}, bf16[40,2688]{1,0:T(8,128)(2,1)S(1)}, u32[]{:S(2)}, u32[]{:S(2)}) collective-permute-start(bf16[40,2688]{1,0:T(8,128)(2,1)S(1)} %get-tuple-element.171), channel_id=1, source_target_pairs={{0,4},{1,5},{2,6},{3,7},{4,8},{5,9},{6,10},{7,11},{8,12},{9,13},{1... | collective-permute-start | bytes 645128 | tf_op jit(solution)/shard_map/ppermute | solution.py:723
  (53 other events, 827.6 us)
Sparse Core Ops, SparseCore 0:
  10.3 104.7 all-gather.2
  316.9 114.9 reduce-scatter.1
